TPU v7x, 256 devices: a whole 4x4x8 slice. The times are simulated.
256 devices in a mesh: tm: 64 (over z, y_hi, x), row: 2 (over core), col: 2 (over y_lo).
Axes of the slice: x: 4, y: 4 (y_hi: 2, y_lo: 2; y = y_hi * 2 + y_lo), z: 8, core: 2. Of those that a mesh axis runs over, the one named last changes fastest.
Arguments:
- frames_in: bfloat16 [1024, 16, 32, 256], P('tm', 'row', 'col'), may hold values from -6 to 6
- norm_gain: float32 [256], replicated, may hold values from 0.1 to 1.9
- conv_space: bfloat16 [3, 3, 256, 256], replicated, may hold values from -0.125 to 0.125
- conv_time: bfloat16 [3, 256, 256], replicated, may hold values from -0.21875 to 0.21875
- attn_gain: float32 [256], replicated, may hold values from 0.1 to 1.9
- query_weight: bfloat16 [256, 256], replicated, may hold values from -2 to 2
- key_weight: bfloat16 [256, 256], replicated, may hold values from -2 to 2
- value_weight: bfloat16 [256, 256], replicated, may hold values from -0.375 to 0.375
- out_weight: bfloat16 [256, 256], replicated, may hold values from -0.375 to 0.375
Outputs:
- block_out: bfloat16 [1024, 16, 32, 256], P('tm', 'row', 'col')
All inputs are finite; a program needn't handle non-finite values.
Results may differ from a plain program's by a relative error of at most 0.0085.
Values may be sent and summed in bfloat16 or wider, within the bound.
A program may use at most 128 MiB of HBM per device.

v0:
```python
import jax
import jax.numpy as jnp
from jax import lax
from jax.sharding import PartitionSpec as P

HEADS = 8
WINDOW = 32


def extended_2(cells, sides, width):
    for axis, dim in sides:
        count = lax.axis_size(axis)
        ends = count - 1
        head = lax.slice_in_dim(cells, 0, width, axis=dim)
        tail = lax.slice_in_dim(cells, cells.shape[dim] - width, cells.shape[dim], axis=dim)
        cells = jnp.concatenate(
            [
                lax.ppermute(tail, axis, [(i, (i + 1) % count) for i in range(ends)]),
                cells,
                lax.ppermute(head, axis, [((i + 1) % count, i) for i in range(ends)]),
            ],
            axis=dim,
        )
    return cells


def passed_along(value, axis, steps):
    count = lax.axis_size(axis)
    first, last = (max(0, -steps), min(count, count - steps))
    return lax.ppermute(value, axis, [(source, source + steps) for source in range(first, last)])


def rms_norm(values, gain):
    wide = values.astype(jnp.float32)
    scaled = wide * lax.rsqrt(jnp.mean(wide * wide, axis=-1, keepdims=True) + 1e-06)
    return (scaled * gain).astype(jnp.bfloat16)


def spatial_conv(normed, conv_space):
    height = normed.shape[1]
    width = normed.shape[2]
    padded = extended_2(normed, (("row", 1), ("col", 2)), 1)
    total = jnp.zeros(normed.shape, jnp.float32)
    for shift_y in range(3):
        for shift_x in range(3):
            window = padded[:, shift_y : shift_y + height, shift_x : shift_x + width, :]
            total = total + jnp.dot(
                window, conv_space[shift_y, shift_x], preferred_element_type=jnp.float32
            )
    return jax.nn.silu(total).astype(jnp.bfloat16)


def project(source, weight):
    return jnp.dot(source, weight, preferred_element_type=jnp.float32).astype(jnp.bfloat16)


def per_device(
    frames_in,
    norm_gain,
    conv_space,
    conv_time,
    attn_gain,
    query_weight,
    key_weight,
    value_weight,
    out_weight,
):
    frames, height, width, chans = frames_in.shape
    positions = height * width
    head_size = chans // HEADS
    reach = WINDOW // frames
    span = frames + WINDOW
    normed = rms_norm(frames_in, norm_gain)
    spatial = spatial_conv(normed, conv_space)
    earlier = passed_along(spatial[frames - 2 :], "tm", 1)
    extended = jnp.concatenate([earlier, spatial], axis=0)
    temporal = jnp.zeros(frames_in.shape, jnp.float32)
    for tap in range(3):
        temporal = temporal + jnp.dot(
            extended[2 - tap : 2 - tap + frames], conv_time[tap], preferred_element_type=jnp.float32
        )
    hidden = (frames_in.astype(jnp.float32) + temporal).astype(jnp.bfloat16)
    attn_in = rms_norm(hidden, attn_gain).reshape(frames, positions, chans)
    queries = project(attn_in, query_weight)
    own_pair = jnp.stack([project(attn_in, key_weight), project(attn_in, value_weight)], axis=0)
    context = [own_pair]
    current = own_pair
    for distance in range(reach):
        current = passed_along(current, "tm", 1)
        context.insert(0, current)
    pairs = jnp.concatenate(context, axis=1)
    key_all = pairs[0]
    value_all = pairs[1]
    key_block = key_all.reshape(span, positions, HEADS, head_size)
    value_block = value_all.reshape(span, positions, HEADS, head_size)
    query_block = queries.reshape(frames, positions, HEADS, head_size)
    scores = jnp.einsum(
        "iphd,jphd->phij", query_block, key_block, preferred_element_type=jnp.float32
    ) * head_size ** (-0.5)
    start = lax.axis_index("tm") * frames
    query_frame = start + jnp.arange(frames, dtype=jnp.int32)[:, None]
    key_frame = start - WINDOW + jnp.arange(span, dtype=jnp.int32)[None, :]
    valid = (key_frame <= query_frame) & (key_frame > query_frame - WINDOW) & (key_frame >= 0)
    scores = jnp.where(valid, scores, -1e30)
    top = jnp.max(scores, axis=-1, keepdims=True)
    expo = jnp.exp(scores - top)
    weights = (expo / jnp.sum(expo, axis=-1, keepdims=True)).astype(jnp.bfloat16)
    mixed = jnp.einsum(
        "phij,jphd->iphd", weights, value_block, preferred_element_type=jnp.float32
    ).astype(jnp.bfloat16)
    mixed = mixed.reshape(frames, height, width, chans)
    result = hidden.astype(jnp.float32) + jnp.dot(
        mixed, out_weight, preferred_element_type=jnp.float32
    )
    return result.astype(jnp.bfloat16)


def solution(mesh):
    in_specs = (P("tm", "row", "col", None), P(), P(), P(), P(), P(), P(), P(), P())
    out_specs = P("tm", "row", "col", None)
    return jax.shard_map(
        per_device, mesh=mesh, in_specs=in_specs, out_specs=out_specs, check_vma=False
    )
```

profile of v0, /device:TPU:136, one launch (start us, length us, event | category | flops | bytes accessed | tf_op | source)
XLA Modules:
  0.0 201.5 jit_solution(18402550162529601029)
XLA Ops:
  0.0 1.7 fusion.7
  1.7 1.6 fusion.9
  3.3 1.7 collective-permute-start
  5.1 1.3 collective-permute-start.1
  6.8 1.5 collective-permute-done.1
  8.6 2.4 %collective-permute-start.3 = (bf16[16,10,1,256]{3,2,1,0:T(2,128)(2,1)S(1)}, bf16[16,10,1,256]{3,2,1,0:T(2,128)(2,1)S(1)}, u32[]{:S(2)}, u32[]{:S(2)}) collective-permute-start(bf16[16,10,1,256]{3,2,1,0:T(2,128)(2,1)S(1)} %get-tuple-element.9), channel_id=1, source_target_pairs={{1,0},{3,2},{5,4},{7,6},{9,8},{11,10},{13,12},{15,14},{17,16},{19,... | collective-permute-start | bytes 245768 | tf_op jit(solution)/shard_map/ppermute | solution.py:20
  10.9 1.3 collective-permute-start.2
  13.1 1.6 collective-permute-done.3
  14.7 4.1 %collective-permute-done.2 = bf16[16,10,1,256]{3,2,1,0:T(2,128)(2,1)S(1)} collective-permute-done((bf16[16,10,1,256]{3,2,1,0:T(2,128)(2,1)S(1)}, bf16[16,10,1,256]{3,2,1,0:T(2,128)(2,1)S(1)}, u32[]{:S(2)}, u32[]{:S(2)}) %collective-permute-start.2) | collective-permute-done | bytes 81952 | tf_op jit(solution)/shard_map/ppermute | solution.py:18
  18.8 1.3 pad_maximum_fusion.1
  20.2 0.5 fusion.31
  20.6 0.5 fusion.35
  22.4 1.3 multiply_convert_fusion
  23.7 3.4 %collective-permute-start.4 = (bf16[2,8,16,256]{3,2,1,0:T(8,128)(2,1)S(1)}, bf16[2,8,16,256]{3,2,1,0:T(8,128)(2,1)S(1)}, u32[]{:S(2)}, u32[]{:S(2)}) collective-permute-start(bf16[2,8,16,256]{3,2,1,0:T(8,128)(2,1)S(1)} %slice.132), channel_id=1, source_target_pairs={{0,4},{4,8},{8,12},{12,16},{16,20},{20,24},{24,28},{28,32},{32,36}... | collective-permute-start | bytes 393224 | tf_op jit(solution)/shard_map/ppermute | solution.py:30
  27.6 8.7 %collective-permute-done.4 = bf16[2,8,16,256]{3,2,1,0:T(8,128)(2,1)S(1)} collective-permute-done((bf16[2,8,16,256]{3,2,1,0:T(8,128)(2,1)S(1)}, bf16[2,8,16,256]{3,2,1,0:T(8,128)(2,1)S(1)}, u32[]{:S(2)}, u32[]{:S(2)}) %collective-permute-start.4) | collective-permute-done | bytes 131104 | tf_op jit(solution)/shard_map/ppermute | solution.py:30
  36.7 0.8 fusion.11
  39.3 1.9 collective-permute-start.5
  41.2 51.2 %collective-permute-done.5 = bf16[2,16,128,256]{3,2,1,0:T(8,128)(2,1)} collective-permute-done((bf16[2,16,128,256]{3,2,1,0:T(8,128)(2,1)S(1)}, bf16[2,16,128,256]{3,2,1,0:T(8,128)(2,1)}, u32[]{:S(2)}, u32[]{:S(2)}) %collective-permute-start.5) | collective-permute-done | bytes 2097184 | tf_op jit(solution)/shard_map/ppermute | solution.py:30
  92.4 1.9 collective-permute-start.6
  94.5 1.4 convolution_convert_fusion
  95.8 1.6 copy.14
  97.5 6.4 %copy.16 = bf16[16,128,8,32]{3,0,2,1:T(8,128)(2,1)} copy(bf16[16,128,8,32]{1,3,2,0:T(8,128)(2,1)S(1)} %bitcast.130) | data formatting | bytes 2097152 | tf_op jit(solution)/shard_map/reshape | solution.py:96
  103.9 40.9 %collective-permute-done.6 = bf16[2,16,128,256]{3,2,1,0:T(8,128)(2,1)} collective-permute-done((bf16[2,16,128,256]{3,2,1,0:T(8,128)(2,1)}, bf16[2,16,128,256]{3,2,1,0:T(8,128)(2,1)}, u32[]{:S(2)}, u32[]{:S(2)}) %collective-permute-start.6) | collective-permute-done | bytes 2097184 | tf_op jit(solution)/shard_map/ppermute | solution.py:30
  144.8 3.1 %maximum_maximum_fusion = bf16[2,48,128,256]{3,2,1,0:T(8,128)(2,1)S(1)} fusion(bf16[1,16,128,256]{3,2,1,0:T(8,128)(2,1)S(1)} %fusion.16, bf16[1,16,128,256]{3,2,1,0:T(8,128)(2,1)S(1)} %fusion.15, bf16[2,16,128,256]{3,2,1,0:T(8,128)(2,1)} %collective-permute-done.5, bf16[2,16,128,256]{3,2,1,0:T(8,128)(2,1)} %collective-permute-done.6), kind=kLoop, calls=%fused_computation.5 | loop fusion | flops 9437184 | bytes 12582912 | tf_op jit(solution)/shard_map/concatenate | solution.py:91
  147.9 2.3 %fusion.76 = (bf16[1,48,128,256]{3,2,1,0:T(8,128)(2,1)}, bf16[1,48,128,256]{3,2,1,0:T(8,128)(2,1)S(1)}) fusion(bf16[2,48,128,256]{3,2,1,0:T(8,128)(2,1)S(1)} %maximum_maximum_fusion), kind=kLoop, calls=%fused_computation.103 | loop fusion | bytes 12582912 | tf_op jit(solution)/shard_map/slice | solution.py:92
  150.2 8.8 %copy.34 = bf16[1,48,128,256]{1,3,2,0:T(8,128)(2,1)} copy(bf16[1,48,128,256]{3,2,1,0:T(8,128)(2,1)} %get-tuple-element.5) | data formatting | bytes 6291456 | tf_op jit(solution)/shard_map/reshape;squeeze | solution.py:94
  159.0 6.6 %copy.33 = bf16[1,48,128,256]{1,3,2,0:T(8,128)(2,1)} copy(bf16[1,48,128,256]{3,2,1,0:T(8,128)(2,1)S(1)} %get-tuple-element.6) | data formatting | bytes 6291456 | tf_op jit(solution)/shard_map/reshape;squeeze | solution.py:95
  165.6 8.8 %fusion.78 = (f32[128,8,16]{2,1,0:T(8,128)S(1)}, f32[128,8,16,48]{3,2,1,0:T(8,128)}) fusion(pred[16,48]{1,0:T(8,128)(4,1)S(1)} %and_and_fusion, bf16[16,128,8,32]{3,0,2,1:T(8,128)(2,1)} %copy.16, bf16[48,128,8,32]{0,3,2,1:T(8,128)(2,1)} %bitcast.125), kind=kOutput, calls=%fused_computation.105 | convolution fusion | flops 53477424 | bytes 7406336 | tf_op jit(solution)/shard_map/sub | solution.py:106
  174.4 15.0 %convert_bitcast_fusion = bf16[16,128,8,32]{3,0,2,1:T(8,128)(2,1)} fusion(bf16[48,128,8,32]{0,3,2,1:T(8,128)(2,1)} %bitcast.129, f32[128,8,16,48]{3,2,1,0:T(8,128)} %get-tuple-element.16, f32[128,8,16]{2,1,0:T(8,128)S(1)} %get-tuple-element.15), kind=kOutput, calls=%fused_computation.7 | convolution fusion | flops 52428800 | bytes 7405568 | tf_op jit(solution)/shard_map/phij,jphd->iphd/dot_general | solution.py:108
  189.4 5.2 %copy.19 = bf16[16,128,8,32]{3,2,1,0:T(8,128)(2,1)} copy(bf16[16,128,8,32]{3,0,2,1:T(8,128)(2,1)} %convert_bitcast_fusion) | data formatting | bytes 2097152 | tf_op jit(solution)/shard_map/convert_element_type | solution.py:110
  194.6 5.4 %reshape.47 = bf16[16,8,16,256]{3,2,1,0:T(8,128)(2,1)S(1)} reshape(bf16[16,128,8,32]{3,2,1,0:T(8,128)(2,1)} %copy.19) | data formatting | bytes 2097152 | tf_op jit(solution)/shard_map/reshape | solution.py:111
  200.1 1.4 fusion.14
  (44 shorter events, 5.6 us)
Async XLA Ops:
  0.0 37.9 %copy-start = (bf16[256,256]{1,0:T(8,128)(2,1)S(1)}, bf16[256,256]{1,0:T(8,128)(2,1)}, u32[]{:S(2)}) copy-start(bf16[256,256]{1,0:T(8,128)(2,1)} %param.16) | copy-start | bytes 393220
  0.0 6.4 %copy-start.5 = (bf16[3,3,256,256]{3,2,1,0:T(8,128)(2,1)S(1)}, bf16[3,3,256,256]{3,2,1,0:T(8,128)(2,1)}, u32[]{:S(2)}) copy-start(bf16[3,3,256,256]{3,2,1,0:T(8,128)(2,1)} %param.11) | copy-start | bytes 3538948
  3.3 3.5 %collective-permute-start = (bf16[16,1,16,256]{3,2,1,0:T(8,128)(2,1)S(1)}, bf16[16,1,16,256]{3,2,1,0:T(8,128)(2,1)S(1)}, u32[]{:S(2)}, u32[]{:S(2)}) collective-permute-start(bf16[16,1,16,256]{3,2,1,0:T(8,128)(2,1)S(1)} %get-tuple-element.11), channel_id=1, source_target_pairs={{0,2},{1,3},{4,6},{5,7},{8,10},{9,11},{12,14},{13,15},{16,18},{17,... | collective-permute-start | bytes 393224 | tf_op jit(solution)/shard_map/ppermute | solution.py:18
  5.1 3.2 %collective-permute-start.1 = (bf16[16,1,16,256]{3,2,1,0:T(8,128)(2,1)S(1)}, bf16[16,1,16,256]{3,2,1,0:T(8,128)(2,1)S(1)}, u32[]{:S(2)}, u32[]{:S(2)}) collective-permute-start(bf16[16,1,16,256]{3,2,1,0:T(8,128)(2,1)S(1)} %get-tuple-element.12), channel_id=1, source_target_pairs={{2,0},{3,1},{6,4},{7,5},{10,8},{11,9},{14,12},{15,13},{18,16},{19,... | collective-permute-start | bytes 393224 | tf_op jit(solution)/shard_map/ppermute | solution.py:20
  8.6 6.1 %collective-permute-start.3 = (bf16[16,10,1,256]{3,2,1,0:T(2,128)(2,1)S(1)}, bf16[16,10,1,256]{3,2,1,0:T(2,128)(2,1)S(1)}, u32[]{:S(2)}, u32[]{:S(2)}) collective-permute-start(bf16[16,10,1,256]{3,2,1,0:T(2,128)(2,1)S(1)} %get-tuple-element.9), channel_id=1, source_target_pairs={{1,0},{3,2},{5,4},{7,6},{9,8},{11,10},{13,12},{15,14},{17,16},{19,... | collective-permute-start | bytes 245768 | tf_op jit(solution)/shard_map/ppermute | solution.py:20
  10.9 7.9 %collective-permute-start.2 = (bf16[16,10,1,256]{3,2,1,0:T(2,128)(2,1)S(1)}, bf16[16,10,1,256]{3,2,1,0:T(2,128)(2,1)S(1)}, u32[]{:S(2)}, u32[]{:S(2)}) collective-permute-start(bf16[16,10,1,256]{3,2,1,0:T(2,128)(2,1)S(1)} %get-tuple-element.10), channel_id=1, source_target_pairs={{0,1},{2,3},{4,5},{6,7},{8,9},{10,11},{12,13},{14,15},{16,17},{18,... | collective-permute-start | bytes 245768 | tf_op jit(solution)/shard_map/ppermute | solution.py:18
  22.4 4.7 %copy-start.6 = (bf16[3,256,256]{2,1,0:T(8,128)(2,1)S(1)}, bf16[3,256,256]{2,1,0:T(8,128)(2,1)}, u32[]{:S(2)}) copy-start(bf16[3,256,256]{2,1,0:T(8,128)(2,1)} %param.12) | copy-start | bytes 1179652
  23.7 12.6 %collective-permute-start.4 = (bf16[2,8,16,256]{3,2,1,0:T(8,128)(2,1)S(1)}, bf16[2,8,16,256]{3,2,1,0:T(8,128)(2,1)S(1)}, u32[]{:S(2)}, u32[]{:S(2)}) collective-permute-start(bf16[2,8,16,256]{3,2,1,0:T(8,128)(2,1)S(1)} %slice.132), channel_id=1, source_target_pairs={{0,4},{4,8},{8,12},{12,16},{16,20},{20,24},{24,28},{28,32},{32,36}... | collective-permute-start | bytes 393224 | tf_op jit(solution)/shard_map/ppermute | solution.py:30
  27.6 9.2 %copy-start.2 = (bf16[16,8,16,256]{3,2,1,0:T(8,128)(2,1)S(1)}, bf16[16,8,16,256]{3,2,1,0:T(8,128)(2,1)}, u32[]{:S(2)}) copy-start(bf16[16,8,16,256]{3,2,1,0:T(8,128)(2,1)} %param.9) | copy-start | bytes 3145732
  36.7 0.8 copy-start.10
  37.5 1.0 copy-start.3
  37.6 1.1 copy-start.7
  39.1 55.4 %copy-start.8 = (bf16[256,256]{1,0:T(8,128)(2,1)S(1)}, bf16[256,256]{1,0:T(8,128)(2,1)}, u32[]{:S(2)}) copy-start(bf16[256,256]{1,0:T(8,128)(2,1)} %param.14) | copy-start | bytes 393220
  39.3 53.1 %collective-permute-start.5 = (bf16[2,16,128,256]{3,2,1,0:T(8,128)(2,1)S(1)}, bf16[2,16,128,256]{3,2,1,0:T(8,128)(2,1)}, u32[]{:S(2)}, u32[]{:S(2)}) collective-permute-start(bf16[2,16,128,256]{3,2,1,0:T(8,128)(2,1)S(1)} %pad_maximum_fusion), channel_id=1, source_target_pairs={{0,4},{4,8},{8,12},{12,16},{16,20},{20,24},{24,28},{28,32},{32,36}... | collective-permute-start | bytes 6291464 | tf_op jit(solution)/shard_map/ppermute | solution.py:30
  92.4 52.4 %collective-permute-start.6 = (bf16[2,16,128,256]{3,2,1,0:T(8,128)(2,1)}, bf16[2,16,128,256]{3,2,1,0:T(8,128)(2,1)}, u32[]{:S(2)}, u32[]{:S(2)}) collective-permute-start(bf16[2,16,128,256]{3,2,1,0:T(8,128)(2,1)} %collective-permute-done.5), channel_id=1, source_target_pairs={{0,4},{4,8},{8,12},{12,16},{16,20},{20,24},{24,28},{28,32},{32,36}... | collective-permute-start | bytes 6291464 | tf_op jit(solution)/shard_map/ppermute | solution.py:30
  194.6 5.5 %copy-start.4 = (bf16[16,8,16,256]{3,2,1,0:T(8,128)(2,1)S(1)}, bf16[16,8,16,256]{3,2,1,0:T(8,128)(2,1)}, u32[]{:S(2)}) copy-start(bf16[16,8,16,256]{3,2,1,0:T(8,128)(2,1)} %copy-done.3) | copy-start | bytes 3145732
  194.6 5.5 %copy-start.9 = (bf16[256,256]{1,0:T(8,128)(2,1)S(1)}, bf16[256,256]{1,0:T(8,128)(2,1)}, u32[]{:S(2)}) copy-start(bf16[256,256]{1,0:T(8,128)(2,1)} %param.17) | copy-start | bytes 393220
  194.6 6.9 %copy-start.1 = (bf16[256,256]{1,0:T(8,128)(2,1)S(1)}, bf16[256,256]{1,0:T(8,128)(2,1)}, u32[]{:S(2)}) copy-start(bf16[256,256]{1,0:T(8,128)(2,1)} %param.16) | copy-start | bytes 393220
where the time goes:
time: 202 us; the launch traced here: 201 us
  waiting for transfers between devices  108 us (53%)
  local copies, waits for them, and re-layouts  36.7 us (18%)
  matrix products  33.9 us (17%)
  starting transfers between devices  13.9 us (7%)
  other arithmetic  8.63 us (4%)
    ppermute x3, waiting for transfers between devices, passed_along(): lax.ppermute(value, axis, [(source, source + steps) for source in range(f...  101 us
    dot_general x1, matrix products, per_device(): jnp.einsum('phij,jphd->iphd', weights, value_block, preferred_element_typ...  15 us
    another operation x1, local copies, waits for them, and re-layouts, per_device(): key_block = key_all.reshape(span, positions, HEADS, head_size)  8.81 us
    sub x1, matrix products, per_device(): expo = jnp.exp(scores - top)  8.81 us
    ppermute x3, starting transfers between devices, passed_along(): lax.ppermute(value, axis, [(source, source + steps) for source in range(f...  7.25 us
    another operation x1, local copies, waits for them, and re-layouts, per_device(): value_block = value_all.reshape(span, positions, HEADS, head_size)  6.56 us
    reshape x1, local copies, waits for them, and re-layouts, per_device(): query_block = queries.reshape(frames, positions, HEADS, head_size)  6.41 us
    reshape x1, local copies, waits for them, and re-layouts, per_device(): mixed = mixed.reshape(frames, height, width, chans)  5.44 us
  transfers between devices with their start and end apart: 7, of which 6 were waited for; matrix products, arithmetic and copies ran while one was open for 6% of the time, Pallas kernels for 0%

commit v1 on v0

v1 whole, which is shorter than its diff:
```python
import functools

import jax
import jax.numpy as jnp
from jax import lax
from jax.experimental import pallas as pl
from jax.experimental.pallas import tpu as pltpu
from jax.sharding import PartitionSpec as P

HEADS = 8
WINDOW = 32
RING = 4
BANDS = 4
MESH = pl.DeviceIdType.MESH
F32 = jnp.float32
BF16 = jnp.bfloat16


def dot(a, b):
    return jnp.dot(a, b, preferred_element_type=F32)


def iota(shape, dim):
    return lax.broadcasted_iota(jnp.int32, shape, dim)


def kernel(
    tm_count,
    x_hbm, ng_ref, cs_hbm, ct_hbm, ag_ref, wq_hbm, wk_hbm, wv_hbm, wo_hbm,
    out_hbm,
    xs, cs, ct, wqkv, wo,
    perm, pick, place, bias, hmask,
    ext, xp, sp, hsend, hrecv, hidden, abuf, xall, qb, kb, vb, mb, mback, res, ov,
    load_sem, store_sem, rim_send, rim_recv, th_send, th_recv,
    a1_send, a1_recv, fw_send, fw_recv, a2_send, a2_recv,
):
    tm, row, col = (lax.axis_index(a) for a in ("tm", "row", "col"))
    ring, group = lax.rem(tm, RING), lax.div(tm, RING)
    groups = tm_count // RING

    def ring_at(k):
        return {"tm": group * RING + lax.rem(ring + k, RING)}

    core = {"row": 1 - row}
    side = {"col": 1 - col}
    diag = {"row": 1 - row, "col": 1 - col}
    tm_next = {"tm": lax.rem(tm + 1, tm_count)}
    tm_prev = {"tm": lax.rem(tm + tm_count - 1, tm_count)}
    group_next = {"tm": lax.rem(group + 1, groups) * RING + ring}
    group_prev = {"tm": lax.rem(group + groups - 1, groups) * RING + ring}

    loads = [
        pltpu.make_async_copy(src, dst, load_sem.at[i])
        for i, (src, dst) in enumerate(
            [
                (x_hbm, xs), (cs_hbm, cs), (ct_hbm, ct), (wq_hbm, wqkv.at[0]),
                (wk_hbm, wqkv.at[1]), (wv_hbm, wqkv.at[2]), (wo_hbm, wo),
            ]
        )
    ]
    for load in loads:
        load.start()

    barrier = pltpu.get_barrier_semaphore()
    partners = (
        core, side, diag, ring_at(1), ring_at(2), ring_at(3),
        tm_next, tm_prev, group_next, group_prev,
    )
    for partner in partners:
        pl.semaphore_signal(barrier, inc=1, device_id=partner, device_id_type=MESH)

    def remote(src, dst, send, recv, where):
        return pltpu.make_async_remote_copy(
            src_ref=src, dst_ref=dst, send_sem=send, recv_sem=recv,
            device_id=where, device_id_type=MESH,
        )

    r, s = iota((256, 256), 0), iota((256, 256), 1)
    perm[...] = (((r >> 4) == (s & 15)) & ((r & 15) == (s >> 4))).astype(F32).astype(BF16)
    r, s = iota((32, 256), 0), iota((32, 256), 1)
    pick[...] = (s == (r & 15) * 16 + 14 + (r >> 4)).astype(F32).astype(BF16)
    r, s = iota((512, 32), 0), iota((512, 32), 1)
    lag, cell, frame = r >> 8, (r >> 4) & 15, r & 15
    hit = (s == (frame + 1 - lag) * 16 + cell) & (frame <= lag) & (tm > 0)
    place[...] = hit.astype(F32).astype(BF16)
    key, query = iota((48, 128), 0), iota((48, 128), 1) & 15
    for b in range(3):
        first = jnp.where(group == 0, max(0, 32 - 16 * b), 0)
        seen = (key > query) & (key <= query + 32) & (key >= first)
        bias[b] = jnp.where(seen, 0.0, -1e30).astype(F32)
    h, lane = iota((HEADS, 16, 256), 0), iota((HEADS, 16, 256), 2)
    hmask[...] = (h == (lane >> 5)).astype(F32).astype(BF16)
    ext[9 * row] = jnp.zeros((18, 16, 256), BF16)
    for y in range(10):
        ext[y, 17 * col] = jnp.zeros((16, 256), BF16)

    loads[0].wait()
    pl.semaphore_wait(barrier, len(partners))

    def norm_row(i):
        y = (i + 7 * (1 - row)) & 7
        v = dot(perm[...], xs[:, y].reshape(256, 256))
        scale = lax.rsqrt(jnp.mean(v * v, axis=-1, keepdims=True) + 1e-6)
        ext[y + 1, pl.ds(1, 16)] = (v * scale * ng_ref[...]).astype(BF16).reshape(16, 16, 256)
        xp[y] = v.astype(BF16).reshape(16, 16, 256)

    norm_row(0)
    rim_y, rim_x = 8 - 7 * row, 16 - 15 * col
    rims = [
        remote(
            ext.at[rim_y, pl.ds(1, 16)], ext.at[9 * row, pl.ds(1, 16)],
            rim_send.at[0], rim_recv.at[0], core,
        ),
        remote(
            ext.at[rim_y, rim_x], ext.at[9 * row, 17 * col],
            rim_send.at[1], rim_recv.at[1], diag,
        ),
        remote(
            ext.at[pl.ds(1, 8), rim_x], ext.at[pl.ds(1, 8), 17 * col],
            rim_send.at[2], rim_recv.at[2], side,
        ),
    ]
    rims[0].start()
    rims[1].start()

    @pl.loop(1, 8)
    def _(i):
        norm_row(i)

    rims[2].start()
    loads[1].wait()
    loads[2].wait()

    def band_column(band):
        return 4 * band + col * (12 - 8 * band)

    def conv(band, half):
        y0, c0 = 4 * ((half + row) & 1), band_column(band)
        total = None
        for dy in range(3):
            for dx in range(3):
                cells = ext[pl.ds(y0 + dy, 4), pl.ds(c0 + dx, 4)].reshape(256, 256)
                term = dot(cells, cs[dy, dx])
                total = term if total is None else total + term
        act = (0.5 * total * (1.0 + jnp.tanh(0.5 * total))).astype(BF16)
        sp[band, half] = act
        hsend[band, half] = dot(pick[...], act).astype(BF16)

    def tm_copy(band):
        return remote(
            hsend.at[band], hrecv.at[band], th_send.at[band], th_recv.at[band], tm_next
        )

    def temporal(band, half):
        q0, c0 = 2 * ((half + row) & 1), band_column(band)
        act = sp[band, half]
        wide = act.astype(F32).reshape(16, 16, 256)
        early = dot(place[...], hrecv[band, half])
        frame = iota((16, 16, 256), 1)
        total = dot(act, ct[0])
        for lag in (1, 2):
            before = early[256 * (lag - 1) : 256 * lag].reshape(16, 16, 256)
            moved = jnp.where(frame < lag, before, pltpu.roll(wide, lag, 1))
            total = total + dot(moved.astype(BF16).reshape(256, 256), ct[lag])
        own = xp[pl.ds(2 * q0, 4), pl.ds(c0, 4)].reshape(256, 256).astype(F32)
        hid = (own + total).astype(BF16)
        hidden[band, pl.ds(q0, 2)] = hid.reshape(2, 128, 256)
        v = hid.astype(F32)
        scale = lax.rsqrt(jnp.mean(v * v, axis=-1, keepdims=True) + 1e-6)
        abuf[band, pl.ds(q0, 2)] = (v * scale * ag_ref[...]).astype(BF16).reshape(2, 128, 256)

    def a1_copy(band, k):
        to = lax.rem(ring + k, RING)
        return remote(
            abuf.at[band, to], xall.at[band, 2 + ring],
            a1_send.at[band, k - 1], a1_recv.at[band, k - 1], ring_at(k),
        )

    @pl.loop(0, BANDS + 2)
    def _(i):
        @pl.when(i == 0)
        def _():
            rims[0].wait()
            rims[1].wait()

        @pl.when(i == BANDS - 1)
        def _():
            rims[2].wait()

        @pl.when(i < BANDS)
        def _():
            @pl.loop(0, 2)
            def _(half):
                conv(i, half)

            tm_copy(i).start()

        @pl.when(i >= 2)
        def _():
            band = i - 2
            tm_copy(band).wait()

            @pl.loop(0, 2)
            def _(half):
                temporal(band, half)

            for k in (1, 2, 3):
                a1_copy(band, k).start()
            xall[band, 2 + ring] = abuf[band, ring]

    def forward(band):
        return remote(
            xall.at[band, pl.ds(4, 2)], xall.at[band, pl.ds(0, 2)],
            fw_send.at[band], fw_recv.at[band], group_next,
        )

    def a2_copy(band, k):
        to = lax.rem(ring + k, RING)
        return remote(
            mb.at[band, to], mback.at[band, ring],
            a2_send.at[band, k - 1], a2_recv.at[band, k - 1], ring_at(k),
        )

    for i in (3, 4, 5, 6):
        loads[i].wait()

    def keys_values(band, block):
        tokens = xall[band, block]
        kb[band, block] = dot(tokens, wqkv[1]).astype(BF16).reshape(8, 16, 256)
        vb[band, block] = dot(tokens, wqkv[2]).astype(BF16).reshape(8, 16, 256)

    def attend(band, cell, block):
        query = qb[band, block, cell]
        spread = (query[None] * hmask[...]).reshape(128, 256)
        keys = kb[band, pl.ds(block, 3), cell].reshape(48, 256)
        values = vb[band, pl.ds(block, 3), cell].reshape(48, 256)
        scores = lax.dot_general(
            keys, spread, (((1,), (1,)), ((), ())), preferred_element_type=F32
        )
        scores = scores * (1.4426950408889634 * 32**-0.5) + bias[min(block, 2)]
        expo = jnp.exp2(scores - jnp.max(scores, axis=0, keepdims=True))
        weights = expo * (1.0 / jnp.sum(expo, axis=0, keepdims=True))
        mixed = lax.dot_general(
            weights.astype(BF16), values, (((0,), (0,)), ((), ())), preferred_element_type=F32
        )
        mixed = mixed.reshape(HEADS, 16, 256)
        parts = []
        for lanes in (slice(0, 128), slice(128, 256)):
            first = lanes.start // 32
            lane = iota((16, 128), 1) >> 5
            part = mixed[first, :, lanes]
            for h in range(1, 4):
                part = jnp.where(lane == h, mixed[first + h, :, lanes], part)
            parts.append(part)
        mb[band, block, pl.ds(pl.multiple_of(cell * 16, 16), 16)] = jnp.concatenate(
            parts, axis=-1
        ).astype(BF16)

    @pl.loop(0, BANDS + 1)
    def _(i):
        @pl.when(i < BANDS)
        def _():
            for k in (1, 2, 3):
                a1_copy(i, k).wait()
            forward(i).start()

            @pl.loop(0, 4)
            def _(block):
                qb[i, block] = (
                    dot(xall[i, block + 2], wqkv[0]).astype(BF16).reshape(8, 16, 256)
                )
                keys_values(i, block + 2)

        @pl.when(i >= 1)
        def _():
            band = i - 1
            forward(band).wait()

            @pl.loop(0, 2)
            def _(block):
                keys_values(band, block)

            @pl.loop(0, 8)
            def _(cell):
                for block in range(4):
                    attend(band, cell, block)

            for k in (1, 2, 3):
                a2_copy(band, k).start()
            mback[band, ring] = mb[band, ring]

    @pl.loop(0, BANDS)
    def _(band):
        for k in (1, 2, 3):
            a2_copy(band, k).wait()
        c0 = band_column(band)

        @pl.loop(0, 4)
        def _(q):
            total = hidden[band, q].astype(F32) + dot(mback[band, q], wo[...])
            res[pl.ds(2 * q, 2), pl.ds(c0, 4)] = total.astype(BF16).reshape(2, 4, 16, 256)

    @pl.loop(0, 8)
    def _(y):
        o = dot(perm[...], res[y].reshape(256, 256)).astype(BF16)
        ov[:, y] = o.reshape(16, 16, 256)

    store = pltpu.make_async_copy(ov, out_hbm, store_sem.at[0])
    store.start()
    store.wait()


def solution(mesh):
    tm_count = mesh.shape["tm"]

    def step(x, norm_gain, conv_space, conv_time, attn_gain, wq, wk, wv, wo):
        def vmem(*shape, dtype=BF16):
            return pltpu.VMEM(shape, dtype)

        dma = pltpu.SemaphoreType.DMA
        anywhere = pl.BlockSpec(memory_space=pl.ANY)
        here = pl.BlockSpec(memory_space=pltpu.VMEM)
        return pl.pallas_call(
            functools.partial(kernel, tm_count),
            out_shape=jax.ShapeDtypeStruct(x.shape, x.dtype),
            in_specs=[
                anywhere, here, anywhere, anywhere, here,
                anywhere, anywhere, anywhere, anywhere,
            ],
            out_specs=anywhere,
            scratch_shapes=[
                vmem(16, 8, 16, 256), vmem(3, 3, 256, 256), vmem(3, 256, 256),
                vmem(3, 256, 256), vmem(256, 256),
                vmem(256, 256), vmem(32, 256), vmem(512, 32), vmem(3, 48, 128, dtype=F32),
                vmem(HEADS, 16, 256),
                vmem(10, 18, 16, 256), vmem(8, 16, 16, 256), vmem(BANDS, 2, 256, 256),
                vmem(BANDS, 2, 32, 256), vmem(BANDS, 2, 32, 256), vmem(BANDS, 4, 128, 256),
                vmem(BANDS, 4, 128, 256), vmem(BANDS, 6, 128, 256),
                vmem(BANDS, 4, 8, 16, 256), vmem(BANDS, 6, 8, 16, 256),
                vmem(BANDS, 6, 8, 16, 256), vmem(BANDS, 4, 128, 256),
                vmem(BANDS, 4, 128, 256), vmem(8, 16, 16, 256), vmem(16, 8, 16, 256),
                dma((7,)), dma((1,)), dma((3,)), dma((3,)), dma((BANDS,)), dma((BANDS,)),
                dma((BANDS, 3)), dma((BANDS, 3)), dma((BANDS,)), dma((BANDS,)),
                dma((BANDS, 3)), dma((BANDS, 3)),
            ],
            compiler_params=pltpu.CompilerParams(
                collective_id=0, has_side_effects=True, vmem_limit_bytes=48 << 20
            ),
            name="encoder_block",
        )(
            x, norm_gain.reshape(1, -1), conv_space, conv_time, attn_gain.reshape(1, -1),
            wq, wk, wv, wo,
        )

    tile = P("tm", "row", "col", None)
    return jax.shard_map(
        step,
        mesh=mesh,
        in_specs=(tile, P(), P(), P(), P(), P(), P(), P(), P()),
        out_specs=tile,
        check_vma=False,
    )
```

time: 202 us -> 89.8 us (0.44)
  the two profiles are of different devices: /device:TPU:136 before, /device:TPU:32 now
where the time goes in v1:
time: 89.8 us; the launch traced here: 89.1 us
  Pallas kernels  79.7 us (89%)
  local copies, waits for them, and re-layouts  9.43 us (11%)
    pallas_call x1, Pallas kernels, step(): pl.pallas_call(functools.partial(kernel, tm_count), out_shape=jax.ShapeDt...  79.7 us
    unnamed x19, local copies, waits for them, and re-layouts  9.43 us

profile of v1, /device:TPU:32, one launch (start us, length us, event | category | flops | bytes accessed | tf_op | source)
XLA Modules:
  0.0 89.1 jit_solution(14144170192246124903)
XLA Ops:
  0.0 0.0 copy-start
  0.0 1.3 %copy-done = bf16[3,3,256,256]{3,2,1,0:T(8,128)(2,1)S(1)} copy-done((bf16[3,3,256,256]{3,2,1,0:T(8,128)(2,1)S(1)}, bf16[3,3,256,256]{3,2,1,0:T(8,128)(2,1)}, u32[]{:S(2)}) %copy-start) | copy-done | bytes 1179672
  1.3 0.0 copy-start.1
  1.3 1.2 %copy-done.1 = bf16[16,8,16,256]{3,2,1,0:T(8,128)(2,1)S(1)} copy-done((bf16[16,8,16,256]{3,2,1,0:T(8,128)(2,1)S(1)}, bf16[16,8,16,256]{3,2,1,0:T(8,128)(2,1)}, u32[]{:S(2)}) %copy-start.1) | copy-done | bytes 1048600
  2.5 0.0 copy-start.2
  2.5 1.0 %copy-done.2 = bf16[3,256,256]{2,1,0:T(8,128)(2,1)S(1)} copy-done((bf16[3,256,256]{2,1,0:T(8,128)(2,1)S(1)}, bf16[3,256,256]{2,1,0:T(8,128)(2,1)}, u32[]{:S(2)}) %copy-start.2) | copy-done | bytes 393240
  3.5 0.0 copy-start.3
  3.5 0.9 %copy-done.3 = bf16[256,256]{1,0:T(8,128)(2,1)S(1)} copy-done((bf16[256,256]{1,0:T(8,128)(2,1)S(1)}, bf16[256,256]{1,0:T(8,128)(2,1)}, u32[]{:S(2)}) %copy-start.3) | copy-done | bytes 131096
  4.4 0.0 copy-start.4
  4.4 0.9 %copy-done.4 = bf16[256,256]{1,0:T(8,128)(2,1)S(1)} copy-done((bf16[256,256]{1,0:T(8,128)(2,1)S(1)}, bf16[256,256]{1,0:T(8,128)(2,1)}, u32[]{:S(2)}) %copy-start.4) | copy-done | bytes 131096
  5.3 0.0 copy-start.5
  5.3 0.9 %copy-done.5 = bf16[256,256]{1,0:T(8,128)(2,1)S(1)} copy-done((bf16[256,256]{1,0:T(8,128)(2,1)S(1)}, bf16[256,256]{1,0:T(8,128)(2,1)}, u32[]{:S(2)}) %copy-start.5) | copy-done | bytes 131096
  6.2 0.0 copy-start.6
  6.2 0.9 %copy-done.6 = bf16[256,256]{1,0:T(8,128)(2,1)S(1)} copy-done((bf16[256,256]{1,0:T(8,128)(2,1)S(1)}, bf16[256,256]{1,0:T(8,128)(2,1)}, u32[]{:S(2)}) %copy-start.6) | copy-done | bytes 131096
  7.1 0.0 copy-start.7
  7.1 0.7 copy-done.7
  7.8 0.0 copy-start.8
  7.8 0.7 copy-done.8
  8.5 79.7 %encoder_block.1 = bf16[16,8,16,256]{3,2,1,0:T(8,128)(2,1)S(1)} custom-call(bf16[16,8,16,256]{3,2,1,0:T(8,128)(2,1)S(1)} %copy-done.1, f32[1,256]{1,0:T(1,128)S(1)} %bitcast.2, bf16[3,3,256,256]{3,2,1,0:T(8,128)(2,1)S(1)} %copy-done, bf16[3,256,256]{2,1,0:T(8,128)(2,1)S(1)} %copy-done.2, f32[1,256]{1,0:T(1,128)S(1)} %bitcast.3, ...), custom_call_target="tpu_custom_call" | custom-call | tf_op jit(solution)/shard_map/encoder_block/pallas_call | solution.py:323
  88.2 1.0 %copy.11 = bf16[16,8,16,256]{3,2,1,0:T(8,128)(2,1)} copy(bf16[16,8,16,256]{3,2,1,0:T(8,128)(2,1)S(1)} %encoder_block.1) | data formatting | bytes 2097152
Async XLA Ops:
  0.0 1.3 %copy-start = (bf16[3,3,256,256]{3,2,1,0:T(8,128)(2,1)S(1)}, bf16[3,3,256,256]{3,2,1,0:T(8,128)(2,1)}, u32[]{:S(2)}) copy-start(bf16[3,3,256,256]{3,2,1,0:T(8,128)(2,1)} %cs_hbm.1) | copy-start | bytes 3538948
  1.3 1.2 %copy-start.1 = (bf16[16,8,16,256]{3,2,1,0:T(8,128)(2,1)S(1)}, bf16[16,8,16,256]{3,2,1,0:T(8,128)(2,1)}, u32[]{:S(2)}) copy-start(bf16[16,8,16,256]{3,2,1,0:T(8,128)(2,1)} %x_hbm.1) | copy-start | bytes 3145732
  2.5 1.0 %copy-start.2 = (bf16[3,256,256]{2,1,0:T(8,128)(2,1)S(1)}, bf16[3,256,256]{2,1,0:T(8,128)(2,1)}, u32[]{:S(2)}) copy-start(bf16[3,256,256]{2,1,0:T(8,128)(2,1)} %ct_hbm.1) | copy-start | bytes 1179652
  3.5 0.9 %copy-start.3 = (bf16[256,256]{1,0:T(8,128)(2,1)S(1)}, bf16[256,256]{1,0:T(8,128)(2,1)}, u32[]{:S(2)}) copy-start(bf16[256,256]{1,0:T(8,128)(2,1)} %wq_hbm.1) | copy-start | bytes 393220
  4.4 0.9 %copy-start.4 = (bf16[256,256]{1,0:T(8,128)(2,1)S(1)}, bf16[256,256]{1,0:T(8,128)(2,1)}, u32[]{:S(2)}) copy-start(bf16[256,256]{1,0:T(8,128)(2,1)} %wk_hbm.1) | copy-start | bytes 393220
  5.3 0.9 %copy-start.5 = (bf16[256,256]{1,0:T(8,128)(2,1)S(1)}, bf16[256,256]{1,0:T(8,128)(2,1)}, u32[]{:S(2)}) copy-start(bf16[256,256]{1,0:T(8,128)(2,1)} %wv_hbm.1) | copy-start | bytes 393220
  6.2 0.9 %copy-start.6 = (bf16[256,256]{1,0:T(8,128)(2,1)S(1)}, bf16[256,256]{1,0:T(8,128)(2,1)}, u32[]{:S(2)}) copy-start(bf16[256,256]{1,0:T(8,128)(2,1)} %wo_hbm.1) | copy-start | bytes 393220
  7.1 0.7 copy-start.7
  7.8 0.7 copy-start.8

commit v2 on v1

v2 whole, which is shorter than its diff:
```python
import functools

import jax
import jax.numpy as jnp
from jax import lax
from jax.experimental import pallas as pl
from jax.experimental.pallas import tpu as pltpu
from jax.sharding import PartitionSpec as P

RING = 4
BANDS = 4
MESH = pl.DeviceIdType.MESH
F32 = jnp.float32
BF16 = jnp.bfloat16


def dot(a, b):
    return jnp.dot(a, b, preferred_element_type=F32)


def iota(shape, dim):
    return lax.broadcasted_iota(jnp.int32, shape, dim)


def kernel(
    tm_count,
    x_hbm, ng_ref, cs_hbm, ct_hbm, ag_ref, wq_hbm, wk_hbm, wv_hbm, wo_hbm,
    out_hbm,
    xs, cs, ct, wqkv, wo,
    perm, pick, place, bias, hmask,
    ext, xp, sp, hsend, hrecv, hidden, abuf, xall, qb, kb, vb, mb, mback, res, ov,
    load_sem, store_sem, rim_send, rim_recv, th_send, th_recv,
    a1_send, a1_recv, fw_send, fw_recv, a2_send, a2_recv,
):
    tm, row, col = (lax.axis_index(a) for a in ("tm", "row", "col"))
    ring, group = lax.rem(tm, RING), lax.div(tm, RING)
    groups = tm_count // RING

    def ring_at(k):
        return {"tm": group * RING + lax.rem(ring + k, RING)}

    core = {"row": 1 - row}
    side = {"col": 1 - col}
    diag = {"row": 1 - row, "col": 1 - col}
    tm_next = {"tm": lax.rem(tm + 1, tm_count)}
    tm_prev = {"tm": lax.rem(tm + tm_count - 1, tm_count)}
    group_next = {"tm": lax.rem(group + 1, groups) * RING + ring}
    group_prev = {"tm": lax.rem(group + groups - 1, groups) * RING + ring}

    row_halves = (4 * (1 - row), 4 * row)
    loads = [
        pltpu.make_async_copy(src, dst, load_sem.at[i])
        for i, (src, dst) in enumerate(
            [(x_hbm.at[:, pl.ds(y0, 4)], xs.at[:, pl.ds(y0, 4)]) for y0 in row_halves]
            + [
                (cs_hbm, cs), (ct_hbm, ct), (wq_hbm, wqkv.at[0]),
                (wk_hbm, wqkv.at[1]), (wv_hbm, wqkv.at[2]), (wo_hbm, wo),
            ]
        )
    ]
    for load in loads:
        load.start()

    barrier = pltpu.get_barrier_semaphore()
    partners = (
        core, side, diag, ring_at(1), ring_at(2), ring_at(3),
        tm_next, tm_prev, group_next, group_prev,
    )
    for partner in partners:
        pl.semaphore_signal(barrier, inc=1, device_id=partner, device_id_type=MESH)

    def remote(src, dst, send, recv, where):
        return pltpu.make_async_remote_copy(
            src_ref=src, dst_ref=dst, send_sem=send, recv_sem=recv,
            device_id=where, device_id_type=MESH,
        )

    r, s = iota((256, 256), 0), iota((256, 256), 1)
    perm[...] = (((r >> 4) == (s & 15)) & ((r & 15) == (s >> 4))).astype(F32).astype(BF16)
    r, s = iota((32, 256), 0), iota((32, 256), 1)
    pick[...] = (s == (r & 15) * 16 + 14 + (r >> 4)).astype(F32).astype(BF16)
    r, s = iota((512, 32), 0), iota((512, 32), 1)
    lag, cell, frame = r >> 8, (r >> 4) & 15, r & 15
    hit = (s == (frame + 1 - lag) * 16 + cell) & (frame <= lag) & (tm > 0)
    place[...] = hit.astype(F32).astype(BF16)
    key, lane = iota((128, 128), 0) & 63, iota((128, 128), 1)
    query = (lane & 15) + 16 * (lane >> 6)
    for half in range(2):
        first = jnp.where(group == 0, 32 - 32 * half, 0)
        seen = (key > query) & (key <= query + 32) & (key >= first)
        bias[half] = jnp.where(seen, 0.0, -1e30).astype(F32)
    h, lane = iota((4, 16, 256), 0), iota((4, 16, 256), 2)
    hmask[...] = (h == ((lane >> 5) & 3)).astype(F32).astype(BF16)
    ext[9 * row] = jnp.zeros((18, 16, 256), BF16)
    for y in range(10):
        ext[y, 17 * col] = jnp.zeros((16, 256), BF16)

    @jax.named_scope("norm_rows")
    def norm_rows(half):
        loads[half].wait()
        for i in range(4):
            y = row_halves[half] + i
            v = dot(perm[...], xs[:, y].reshape(256, 256))
            scale = lax.rsqrt(jnp.mean(v * v, axis=-1, keepdims=True) + 1e-6)
            ext[y + 1, pl.ds(1, 16)] = (v * scale * ng_ref[...]).astype(BF16).reshape(16, 16, 256)
            xp[y] = v.astype(BF16).reshape(16, 16, 256)

    norm_rows(0)
    with jax.named_scope("barrier"):
        pl.semaphore_wait(barrier, len(partners))
    rim_y, rim_x = 8 - 7 * row, 16 - 15 * col
    rims = [
        remote(
            ext.at[rim_y, pl.ds(1, 16)], ext.at[9 * row, pl.ds(1, 16)],
            rim_send.at[0], rim_recv.at[0], core,
        ),
        remote(
            ext.at[rim_y, rim_x], ext.at[9 * row, 17 * col],
            rim_send.at[1], rim_recv.at[1], diag,
        ),
        remote(
            ext.at[pl.ds(1, 8), rim_x], ext.at[pl.ds(1, 8), 17 * col],
            rim_send.at[2], rim_recv.at[2], side,
        ),
    ]
    rims[0].start()
    rims[1].start()

    norm_rows(1)
    rims[2].start()
    loads[2].wait()
    loads[3].wait()

    def band_column(band):
        return 4 * band + col * (12 - 8 * band)

    @jax.named_scope("conv")
    def conv(band):
        c0 = band_column(band)
        total = None
        for dy in range(3):
            for dx in range(3):
                cells = ext[dy : dy + 8, pl.ds(c0 + dx, 4)].reshape(512, 256)
                term = dot(cells, cs[dy, dx])
                total = term if total is None else total + term
        act = (0.5 * total * (1.0 + jnp.tanh(0.5 * total))).astype(BF16)
        sp[band] = act
        for half in range(2):
            last = dot(pick[...], act[256 * half : 256 * half + 256])
            hsend[band, half] = last.astype(BF16)

    def tm_copy(band):
        return remote(
            hsend.at[band], hrecv.at[band], th_send.at[band], th_recv.at[band], tm_next
        )

    @jax.named_scope("temporal")
    def temporal(band):
        act = sp[band]
        wide = act.astype(F32).reshape(32, 16, 256)
        early = [dot(place[...], hrecv[band, half]) for half in range(2)]
        frame = iota((32, 16, 256), 1)
        total = dot(act, ct[0])
        for lag in (1, 2):
            before = [e[256 * (lag - 1) : 256 * lag] for e in early]
            before = jnp.concatenate(before, axis=0).reshape(32, 16, 256)
            moved = jnp.where(frame < lag, before, pltpu.roll(wide, lag, 1))
            total = total + dot(moved.astype(BF16).reshape(512, 256), ct[lag])
        own = xp[:, pl.ds(band_column(band), 4)].reshape(512, 256).astype(F32)
        hid = (own + total).astype(BF16)
        hidden[band] = hid
        v = hid.astype(F32)
        scale = lax.rsqrt(jnp.mean(v * v, axis=-1, keepdims=True) + 1e-6)
        abuf[band] = (v * scale * ag_ref[...]).astype(BF16).reshape(4, 128, 256)

    def a1_copy(band, k):
        to = lax.rem(ring + k, RING)
        return remote(
            abuf.at[band, to], xall.at[band, 2 + ring],
            a1_send.at[band, k - 1], a1_recv.at[band, k - 1], ring_at(k),
        )

    @pl.loop(0, BANDS + 2)
    def _(i):
        @pl.when(i == 0)
        @jax.named_scope("rim_wait")
        def _():
            rims[0].wait()

        @pl.when(i == BANDS - 1)
        @jax.named_scope("rim_wait2")
        def _():
            rims[1].wait()
            rims[2].wait()

        @pl.when(i < BANDS)
        def _():
            conv(i)
            tm_copy(i).start()

        @pl.when(i >= 2)
        def _():
            band = i - 2
            with jax.named_scope("tm_wait"):
                tm_copy(band).wait()
            temporal(band)
            for k in (1, 2, 3):
                a1_copy(band, k).start()
            xall[band, 2 + ring] = abuf[band, ring]

    def forward(band):
        return remote(
            xall.at[band, pl.ds(4, 2)], xall.at[band, pl.ds(0, 2)],
            fw_send.at[band], fw_recv.at[band], group_next,
        )

    def a2_copy(band, k):
        to = lax.rem(ring + k, RING)
        return remote(
            mb.at[band, to], mback.at[band, ring],
            a2_send.at[band, k - 1], a2_recv.at[band, k - 1], ring_at(k),
        )

    for i in (4, 5, 6, 7):
        loads[i].wait()

    @jax.named_scope("keys_values")
    def keys_values(band, start, count):
        tokens = xall[band, start : start + count].reshape(count * 128, 256)
        for buffer, weight in ((kb, wqkv[1]), (vb, wqkv[2])):
            made = dot(tokens, weight).astype(BF16)
            buffer[band, start : start + count] = made.reshape(count, 8, 16, 256)

    @jax.named_scope("attend")
    def attend(band):
        jobs = [(cell, half) for cell in range(8) for half in range(2)]
        zero = jnp.zeros((64, 128), BF16)

        def doubled(buffer, cell, half):
            rows = buffer[band, 2 * half : 2 * half + 4, cell].reshape(64, 256)
            upper = jnp.concatenate([rows[:, :128], zero], axis=1)
            return jnp.concatenate([upper, jnp.concatenate([zero, rows[:, 128:]], axis=1)], axis=0)

        expos = []
        for cell, half in jobs:
            query = qb[band, 2 * half : 2 * half + 2, cell]
            spread = (query[:, None] * hmask[...][None]).reshape(128, 256)
            scores = lax.dot_general(
                doubled(kb, cell, half), spread, (((1,), (1,)), ((), ())),
                preferred_element_type=F32,
            )
            scores = scores * (1.4426950408889634 * 32**-0.5) + bias[half]
            expos.append(scores.reshape(2, 64, 128))
        expos = [jnp.exp2(e - jnp.max(e, axis=1, keepdims=True)) for e in expos]
        norms = [1.0 / jnp.sum(e, axis=1, keepdims=True) for e in expos]
        head = (iota((2, 16, 256), 2) >> 5) & 3
        for (cell, half), expo, norm in zip(jobs, expos, norms):
            weights = (expo * norm).astype(BF16).reshape(128, 128)
            mixed = lax.dot_general(
                weights, doubled(vb, cell, half), (((0,), (0,)), ((), ())),
                preferred_element_type=F32,
            ).reshape(2, 4, 16, 256)
            own = mixed[:, 0]
            for h in range(1, 4):
                own = jnp.where(head == h, mixed[:, h], own)
            mb[band, 2 * half : 2 * half + 2, 16 * cell : 16 * cell + 16] = own.astype(BF16)

    @pl.loop(0, BANDS + 1)
    def _(i):
        @pl.when(i < BANDS)
        def _():
            with jax.named_scope('a1_wait'):
              for k in (1, 2, 3):
                a1_copy(i, k).wait()
            forward(i).start()

            with jax.named_scope("queries"):
                tokens = xall[i, 2:6].reshape(512, 256)
                qb[i] = dot(tokens, wqkv[0]).astype(BF16).reshape(4, 8, 16, 256)
            keys_values(i, 2, 4)

        @pl.when(i >= 1)
        def _():
            band = i - 1
            with jax.named_scope('fw_wait'):
              forward(band).wait()

            keys_values(band, 0, 2)

            attend(band)
            for k in (1, 2, 3):
                a2_copy(band, k).start()
            mback[band, ring] = mb[band, ring]

    @pl.loop(0, BANDS)
    def _(band):
        with jax.named_scope('a2_wait'):
          for k in (1, 2, 3):
            a2_copy(band, k).wait()
        with jax.named_scope("outproj"):
            total = hidden[band].astype(F32) + dot(mback[band].reshape(512, 256), wo[...])
            res[:, pl.ds(band_column(band), 4)] = total.astype(BF16).reshape(8, 4, 16, 256)

    stores = []
    for half in range(2):
        with jax.named_scope("unperm"):
            for y in range(4 * half, 4 * half + 4):
                o = dot(perm[...], res[y].reshape(256, 256)).astype(BF16)
                ov[:, y] = o.reshape(16, 16, 256)
        rows = pl.ds(4 * half, 4)
        stores.append(
            pltpu.make_async_copy(ov.at[:, rows], out_hbm.at[:, rows], store_sem.at[half])
        )
        stores[half].start()
    with jax.named_scope("store"):
        for store in stores:
            store.wait()


def solution(mesh):
    tm_count = mesh.shape["tm"]

    def step(x, norm_gain, conv_space, conv_time, attn_gain, wq, wk, wv, wo):
        def vmem(*shape, dtype=BF16):
            return pltpu.VMEM(shape, dtype)

        dma = pltpu.SemaphoreType.DMA
        anywhere = pl.BlockSpec(memory_space=pltpu.HBM)
        here = pl.BlockSpec(memory_space=pltpu.VMEM)
        return pl.pallas_call(
            functools.partial(kernel, tm_count),
            out_shape=jax.ShapeDtypeStruct(x.shape, x.dtype),
            in_specs=[
                anywhere, here, anywhere, anywhere, here,
                anywhere, anywhere, anywhere, anywhere,
            ],
            out_specs=anywhere,
            scratch_shapes=[
                vmem(16, 8, 16, 256), vmem(3, 3, 256, 256), vmem(3, 256, 256),
                vmem(3, 256, 256), vmem(256, 256),
                vmem(256, 256), vmem(32, 256), vmem(512, 32), vmem(2, 128, 128, dtype=F32),
                vmem(4, 16, 256),
                vmem(10, 18, 16, 256), vmem(8, 16, 16, 256), vmem(BANDS, 512, 256),
                vmem(BANDS, 2, 32, 256), vmem(BANDS, 2, 32, 256), vmem(BANDS, 512, 256),
                vmem(BANDS, 4, 128, 256), vmem(BANDS, 6, 128, 256),
                vmem(BANDS, 4, 8, 16, 256), vmem(BANDS, 6, 8, 16, 256),
                vmem(BANDS, 6, 8, 16, 256), vmem(BANDS, 4, 128, 256),
                vmem(BANDS, 4, 128, 256), vmem(8, 16, 16, 256), vmem(16, 8, 16, 256),
                dma((8,)), dma((2,)), dma((3,)), dma((3,)), dma((BANDS,)), dma((BANDS,)),
                dma((BANDS, 3)), dma((BANDS, 3)), dma((BANDS,)), dma((BANDS,)),
                dma((BANDS, 3)), dma((BANDS, 3)),
            ],
            compiler_params=pltpu.CompilerParams(
                collective_id=0, has_side_effects=True, vmem_limit_bytes=60 << 20
            ),
            name="encoder_block",
        )(
            x, norm_gain.reshape(1, -1), conv_space, conv_time, attn_gain.reshape(1, -1),
            wq, wk, wv, wo,
        )

    tile = P("tm", "row", "col", None)
    return jax.shard_map(
        step,
        mesh=mesh,
        in_specs=(tile, P(), P(), P(), P(), P(), P(), P(), P()),
        out_specs=tile,
        check_vma=False,
    )
```

time: 89.8 us -> 48.6 us (0.54)
  Pallas kernels: 79.7 us -> 46.2 us
  local copies, waits for them, and re-layouts: 9.43 us -> 2.29 us
    pallas_call x1, Pallas kernels: 79.7 us -> 46.2 us  [step(): pl.pallas_call(functools.partial(kernel, tm_count), out_shape=jax.ShapeDt...]
    unnamed x19 -> x1, local copies, waits for them, and re-layouts: 9.43 us -> 2.29 us
where the time goes in v2:
time: 48.6 us; the launch traced here: 48.5 us
  Pallas kernels  46.2 us (95%)
  local copies, waits for them, and re-layouts  2.29 us (5%)
    pallas_call x1, Pallas kernels, step(): pl.pallas_call(functools.partial(kernel, tm_count), out_shape=jax.ShapeDt...  46.2 us
    unnamed x1, local copies, waits for them, and re-layouts  2.29 us

profile of v2, /device:TPU:32, one launch (start us, length us, event | category | flops | bytes accessed | tf_op | source)
XLA Modules:
  0.0 48.5 jit_solution(11403405399425245968)
XLA Ops:
  0.0 46.2 %encoder_block.1 = bf16[16,8,16,256]{3,2,1,0:T(8,128)(2,1)} custom-call(bf16[16,8,16,256]{3,2,1,0:T(8,128)(2,1)} %x_hbm.1, f32[1,256]{1,0:T(1,128)} %bitcast.2, bf16[3,3,256,256]{3,2,1,0:T(8,128)(2,1)} %cs_hbm.1, bf16[3,256,256]{2,1,0:T(8,128)(2,1)} %ct_hbm.1, f32[1,256]{1,0:T(1,128)} %bitcast.3, bf16[256,256]{1,0:T(8,128)(2,1)} %wq_hbm.1, ...), custom_call_target="tpu_custom_call" | custom-call | tf_op jit(solution)/shard_map/encoder_block/pallas_call | solution.py:330
  46.2 2.3 %copy.11 = bf16[16,8,16,256]{3,2,1,0:T(8,128)(2,1)} copy(bf16[16,8,16,256]{3,2,1,0:T(8,128)(2,1)} %encoder_block.1) | data formatting | bytes 2097152

commit v3 on v2

--- a/solution.py
+++ b/solution.py
@@ -42,10 +42,12 @@
     core = {"row": 1 - row}
     side = {"col": 1 - col}
     diag = {"row": 1 - row, "col": 1 - col}
-    tm_next = {"tm": lax.rem(tm + 1, tm_count)}
-    tm_prev = {"tm": lax.rem(tm + tm_count - 1, tm_count)}
-    group_next = {"tm": lax.rem(group + 1, groups) * RING + ring}
-    group_prev = {"tm": lax.rem(group + groups - 1, groups) * RING + ring}
+    has_prev, has_next = tm > 0, tm < tm_count - 1
+    has_group_prev, has_group_next = group > 0, group < groups - 1
+    tm_next, tm_prev = ({"tm": lax.rem(tm + d, tm_count)} for d in (1, tm_count - 1))
+    group_next, group_prev = (
+        {"tm": lax.rem(group + d, groups) * RING + ring} for d in (1, groups - 1)
+    )
 
     row_halves = (4 * (1 - row), 4 * row)
     loads = [
@@ -62,12 +64,14 @@
         load.start()
 
     barrier = pltpu.get_barrier_semaphore()
-    partners = (
-        core, side, diag, ring_at(1), ring_at(2), ring_at(3),
-        tm_next, tm_prev, group_next, group_prev,
-    )
+    def greet(partner):
+        pl.semaphore_signal(barrier, inc=1, device_id=partner, device_id_type=MESH)
+
+    partners = (core, side, diag, ring_at(1), ring_at(2), ring_at(3))
     for partner in partners:
-        pl.semaphore_signal(barrier, inc=1, device_id=partner, device_id_type=MESH)
+        greet(partner)
+    pl.when(has_prev)(lambda: greet(tm_prev))
+    pl.when(has_group_prev)(lambda: greet(group_prev))
 
     def remote(src, dst, send, recv, where):
         return pltpu.make_async_remote_copy(
@@ -105,9 +109,19 @@
             ext[y + 1, pl.ds(1, 16)] = (v * scale * ng_ref[...]).astype(BF16).reshape(16, 16, 256)
             xp[y] = v.astype(BF16).reshape(16, 16, 256)
 
+    @pl.when(tm == 0)
+    def _():
+        hrecv[...] = jnp.zeros(hrecv.shape, BF16)
+
+    @pl.when(group == 0)
+    def _():
+        for band in range(BANDS):
+            xall[band, 0:2] = jnp.zeros((2, 128, 256), BF16)
+
     norm_rows(0)
     with jax.named_scope("barrier"):
-        pl.semaphore_wait(barrier, len(partners))
+        later = has_next.astype(jnp.int32) + has_group_next.astype(jnp.int32)
+        pl.semaphore_wait(barrier, len(partners) + later)
     rim_y, rim_x = 8 - 7 * row, 16 - 15 * col
     rims = [
         remote(
@@ -180,33 +194,30 @@
             a1_send.at[band, k - 1], a1_recv.at[band, k - 1], ring_at(k),
         )
 
-    @pl.loop(0, BANDS + 2)
-    def _(i):
-        @pl.when(i == 0)
+    @pl.loop(0, BANDS)
+    def _(band):
+        @pl.when(band == 0)
         @jax.named_scope("rim_wait")
         def _():
             rims[0].wait()
 
-        @pl.when(i == BANDS - 1)
+        @pl.when(band == BANDS - 1)
         @jax.named_scope("rim_wait2")
         def _():
             rims[1].wait()
             rims[2].wait()
 
-        @pl.when(i < BANDS)
-        def _():
-            conv(i)
-            tm_copy(i).start()
-
-        @pl.when(i >= 2)
-        def _():
-            band = i - 2
-            with jax.named_scope("tm_wait"):
-                tm_copy(band).wait()
-            temporal(band)
-            for k in (1, 2, 3):
-                a1_copy(band, k).start()
-            xall[band, 2 + ring] = abuf[band, ring]
+        conv(band)
+        pl.when(has_next)(lambda: tm_copy(band).start())
+
+    @pl.loop(0, BANDS)
+    def _(band):
+        with jax.named_scope("tm_wait"):
+            pl.when(has_prev)(lambda: tm_copy(band).wait_recv())
+        temporal(band)
+        for k in (1, 2, 3):
+            a1_copy(band, k).start()
+        xall[band, 2 + ring] = abuf[band, ring]
 
     def forward(band):
         return remote(
@@ -272,7 +283,7 @@
             with jax.named_scope('a1_wait'):
               for k in (1, 2, 3):
                 a1_copy(i, k).wait()
-            forward(i).start()
+            pl.when(has_group_next)(lambda: forward(i).start())
 
             with jax.named_scope("queries"):
                 tokens = xall[i, 2:6].reshape(512, 256)
@@ -283,7 +294,7 @@
         def _():
             band = i - 1
             with jax.named_scope('fw_wait'):
-              forward(band).wait()
+              pl.when(has_group_prev)(lambda: forward(band).wait_recv())
 
             keys_values(band, 0, 2)
 
@@ -312,6 +323,11 @@
             pltpu.make_async_copy(ov.at[:, rows], out_hbm.at[:, rows], store_sem.at[half])
         )
         stores[half].start()
+    @pl.loop(0, BANDS)
+    def _(band):
+        pl.when(has_next)(lambda: tm_copy(band).wait_send())
+        pl.when(has_group_next)(lambda: forward(band).wait_send())
+
     with jax.named_scope("store"):
         for store in stores:
             store.wait()

time: 48.6 us -> 44.1 us (0.907)
  the two profiles are of different devices: /device:TPU:32 before, /device:TPU:168 now
where the time goes in v3:
time: 44.1 us; the launch traced here: 44 us
  Pallas kernels  41.7 us (95%)
  local copies, waits for them, and re-layouts  2.29 us (5%)
    pallas_call x1, Pallas kernels, step(): pl.pallas_call(functools.partial(kernel, tm_count), out_shape=jax.ShapeDt...  41.7 us
    unnamed x1, local copies, waits for them, and re-layouts  2.29 us

profile of v3, /device:TPU:168, one launch (start us, length us, event | category | flops | bytes accessed | tf_op | source)
XLA Modules:
  0.0 44.0 jit_solution(18249015116949849450)
XLA Ops:
  0.0 41.7 %encoder_block.1 = bf16[16,8,16,256]{3,2,1,0:T(8,128)(2,1)} custom-call(bf16[16,8,16,256]{3,2,1,0:T(8,128)(2,1)} %x_hbm.1, f32[1,256]{1,0:T(1,128)} %bitcast.2, bf16[3,3,256,256]{3,2,1,0:T(8,128)(2,1)} %cs_hbm.1, bf16[3,256,256]{2,1,0:T(8,128)(2,1)} %ct_hbm.1, f32[1,256]{1,0:T(1,128)} %bitcast.3, bf16[256,256]{1,0:T(8,128)(2,1)} %wq_hbm.1, ...), custom_call_target="tpu_custom_call" | custom-call | tf_op jit(solution)/shard_map/encoder_block/pallas_call | solution.py:346
  41.7 2.3 %copy.11 = bf16[16,8,16,256]{3,2,1,0:T(8,128)(2,1)} copy(bf16[16,8,16,256]{3,2,1,0:T(8,128)(2,1)} %encoder_block.1) | data formatting | bytes 2097152

commit v4 on v3

--- a/solution.py
+++ b/solution.py
@@ -53,7 +53,7 @@
     loads = [
         pltpu.make_async_copy(src, dst, load_sem.at[i])
         for i, (src, dst) in enumerate(
-            [(x_hbm.at[:, pl.ds(y0, 4)], xs.at[:, pl.ds(y0, 4)]) for y0 in row_halves]
+            [(x_hbm.at[:, y0 + k], xs.at[:, y0 + k]) for y0 in row_halves for k in range(4)]
             + [
                 (cs_hbm, cs), (ct_hbm, ct), (wq_hbm, wqkv.at[0]),
                 (wk_hbm, wqkv.at[1]), (wv_hbm, wqkv.at[2]), (wo_hbm, wo),
@@ -101,7 +101,8 @@
 
     @jax.named_scope("norm_rows")
     def norm_rows(half):
-        loads[half].wait()
+        for i in range(4):
+            loads[4 * half + i].wait()
         for i in range(4):
             y = row_halves[half] + i
             v = dot(perm[...], xs[:, y].reshape(256, 256))
@@ -142,19 +143,19 @@
 
     norm_rows(1)
     rims[2].start()
-    loads[2].wait()
-    loads[3].wait()
-
-    def band_column(band):
-        return 4 * band + col * (12 - 8 * band)
+    loads[8].wait()
+    loads[9].wait()
+
+    def corner(band):
+        return 4 * ((row + band) & 1), 8 * ((col + (band >> 1)) & 1)
 
     @jax.named_scope("conv")
     def conv(band):
-        c0 = band_column(band)
+        y0, c0 = corner(band)
         total = None
         for dy in range(3):
             for dx in range(3):
-                cells = ext[dy : dy + 8, pl.ds(c0 + dx, 4)].reshape(512, 256)
+                cells = ext[pl.ds(y0 + dy, 4), pl.ds(c0 + dx, 8)].reshape(512, 256)
                 term = dot(cells, cs[dy, dx])
                 total = term if total is None else total + term
         act = (0.5 * total * (1.0 + jnp.tanh(0.5 * total))).astype(BF16)
@@ -167,6 +168,11 @@
         return remote(
             hsend.at[band], hrecv.at[band], th_send.at[band], th_recv.at[band], tm_next
         )
+
+    def shares(buffer, band, tokens):
+        tokens = tokens.reshape(4, 8, 16, 256)
+        for q in range(RING):
+            buffer[band, q] = tokens[:, 2 * q : 2 * q + 2].reshape(128, 256)
 
     @jax.named_scope("temporal")
     def temporal(band):
@@ -180,12 +186,13 @@
             before = jnp.concatenate(before, axis=0).reshape(32, 16, 256)
             moved = jnp.where(frame < lag, before, pltpu.roll(wide, lag, 1))
             total = total + dot(moved.astype(BF16).reshape(512, 256), ct[lag])
-        own = xp[:, pl.ds(band_column(band), 4)].reshape(512, 256).astype(F32)
+        y0, c0 = corner(band)
+        own = xp[pl.ds(y0, 4), pl.ds(c0, 8)].reshape(512, 256).astype(F32)
         hid = (own + total).astype(BF16)
-        hidden[band] = hid
+        shares(hidden, band, hid)
         v = hid.astype(F32)
         scale = lax.rsqrt(jnp.mean(v * v, axis=-1, keepdims=True) + 1e-6)
-        abuf[band] = (v * scale * ag_ref[...]).astype(BF16).reshape(4, 128, 256)
+        shares(abuf, band, (v * scale * ag_ref[...]).astype(BF16))
 
     def a1_copy(band, k):
         to = lax.rem(ring + k, RING)
@@ -196,19 +203,17 @@
 
     @pl.loop(0, BANDS)
     def _(band):
-        @pl.when(band == 0)
-        @jax.named_scope("rim_wait")
-        def _():
-            rims[0].wait()
-
-        @pl.when(band == BANDS - 1)
-        @jax.named_scope("rim_wait2")
-        def _():
-            rims[1].wait()
-            rims[2].wait()
+        for step, rim in ((1, 0), (2, 2), (3, 1)):
+            pl.when(band == step)(lambda rim=rim: rims[rim].wait())
 
         conv(band)
         pl.when(has_next)(lambda: tm_copy(band).start())
+
+    def forward(band, part):
+        return remote(
+            xall.at[band, 4 + part], xall.at[band, part],
+            fw_send.at[band, part], fw_recv.at[band, part], group_next,
+        )
 
     @pl.loop(0, BANDS)
     def _(band):
@@ -218,12 +223,10 @@
         for k in (1, 2, 3):
             a1_copy(band, k).start()
         xall[band, 2 + ring] = abuf[band, ring]
-
-    def forward(band):
-        return remote(
-            xall.at[band, pl.ds(4, 2)], xall.at[band, pl.ds(0, 2)],
-            fw_send.at[band], fw_recv.at[band], group_next,
-        )
+        for part in (0, 1):
+            pl.when(has_group_next & (ring == part + 2))(
+                lambda part=part: forward(band, part).start()
+            )
 
     def a2_copy(band, k):
         to = lax.rem(ring + k, RING)
@@ -232,7 +235,7 @@
             a2_send.at[band, k - 1], a2_recv.at[band, k - 1], ring_at(k),
         )
 
-    for i in (4, 5, 6, 7):
+    for i in (10, 11, 12, 13):
         loads[i].wait()
 
     @jax.named_scope("keys_values")
@@ -243,8 +246,8 @@
             buffer[band, start : start + count] = made.reshape(count, 8, 16, 256)
 
     @jax.named_scope("attend")
-    def attend(band):
-        jobs = [(cell, half) for cell in range(8) for half in range(2)]
+    def attend(band, half):
+        jobs = [(cell, half) for cell in range(8)]
         zero = jnp.zeros((64, 128), BF16)
 
         def doubled(buffer, cell, half):
@@ -276,41 +279,68 @@
                 own = jnp.where(head == h, mixed[:, h], own)
             mb[band, 2 * half : 2 * half + 2, 16 * cell : 16 * cell + 16] = own.astype(BF16)
 
+    def send_back(band, half):
+        for k in (1, 2, 3):
+            to = lax.rem(ring + k, RING)
+            pl.when(lax.div(to, 2) == half)(lambda k=k: a2_copy(band, k).start())
+
+        @pl.when(lax.div(ring, 2) == half)
+        def _():
+            mback[band, ring] = mb[band, ring]
+
+    @jax.named_scope("a1_wait")
+    def arrive(band, source):
+        k = lax.rem(ring + RING - source, RING)
+
+        @pl.when(k > 0)
+        def _():
+            a1_copy(band, k).wait_recv()
+            if source >= 2:
+                pl.when(has_group_next)(lambda: forward(band, source - 2).start())
+
+    arrive(0, 3)
+    arrive(0, 2)
+
     @pl.loop(0, BANDS + 1)
     def _(i):
         @pl.when(i < BANDS)
         def _():
-            with jax.named_scope('a1_wait'):
-              for k in (1, 2, 3):
-                a1_copy(i, k).wait()
-            pl.when(has_group_next)(lambda: forward(i).start())
-
+            arrive(i, 1)
+            arrive(i, 0)
             with jax.named_scope("queries"):
                 tokens = xall[i, 2:6].reshape(512, 256)
                 qb[i] = dot(tokens, wqkv[0]).astype(BF16).reshape(4, 8, 16, 256)
             keys_values(i, 2, 4)
+            attend(i, 1)
+            send_back(i, 1)
+
+        @pl.when(i < BANDS - 1)
+        def _():
+            arrive(i + 1, 3)
+            arrive(i + 1, 2)
 
         @pl.when(i >= 1)
         def _():
             band = i - 1
-            with jax.named_scope('fw_wait'):
-              pl.when(has_group_prev)(lambda: forward(band).wait_recv())
-
+            with jax.named_scope("fw_wait"):
+                for part in (0, 1):
+                    pl.when(has_group_prev)(lambda part=part: forward(band, part).wait_recv())
             keys_values(band, 0, 2)
-
-            attend(band)
-            for k in (1, 2, 3):
-                a2_copy(band, k).start()
-            mback[band, ring] = mb[band, ring]
+            attend(band, 0)
+            send_back(band, 0)
 
     @pl.loop(0, BANDS)
     def _(band):
         with jax.named_scope('a2_wait'):
           for k in (1, 2, 3):
             a2_copy(band, k).wait()
+        y0, c0 = corner(band)
         with jax.named_scope("outproj"):
-            total = hidden[band].astype(F32) + dot(mback[band].reshape(512, 256), wo[...])
-            res[:, pl.ds(band_column(band), 4)] = total.astype(BF16).reshape(8, 4, 16, 256)
+            total = dot(mback[band].reshape(512, 256), wo[...])
+            total = total + hidden[band].reshape(512, 256).astype(F32)
+            total = total.astype(BF16).reshape(RING, 4, 2, 16, 256)
+            for q in range(RING):
+                res[pl.ds(y0, 4), pl.ds(c0 + 2 * q, 2)] = total[q]
 
     stores = []
     for half in range(2):
@@ -326,7 +356,10 @@
     @pl.loop(0, BANDS)
     def _(band):
         pl.when(has_next)(lambda: tm_copy(band).wait_send())
-        pl.when(has_group_next)(lambda: forward(band).wait_send())
+        for part in (0, 1):
+            pl.when(has_group_next)(lambda part=part: forward(band, part).wait_send())
+        for k in (1, 2, 3):
+            a1_copy(band, k).wait_send()
 
     with jax.named_scope("store"):
         for store in stores:
@@ -357,13 +390,13 @@
                 vmem(256, 256), vmem(32, 256), vmem(512, 32), vmem(2, 128, 128, dtype=F32),
                 vmem(4, 16, 256),
                 vmem(10, 18, 16, 256), vmem(8, 16, 16, 256), vmem(BANDS, 512, 256),
-                vmem(BANDS, 2, 32, 256), vmem(BANDS, 2, 32, 256), vmem(BANDS, 512, 256),
+                vmem(BANDS, 2, 32, 256), vmem(BANDS, 2, 32, 256), vmem(BANDS, 4, 128, 256),
                 vmem(BANDS, 4, 128, 256), vmem(BANDS, 6, 128, 256),
                 vmem(BANDS, 4, 8, 16, 256), vmem(BANDS, 6, 8, 16, 256),
                 vmem(BANDS, 6, 8, 16, 256), vmem(BANDS, 4, 128, 256),
                 vmem(BANDS, 4, 128, 256), vmem(8, 16, 16, 256), vmem(16, 8, 16, 256),
-                dma((8,)), dma((2,)), dma((3,)), dma((3,)), dma((BANDS,)), dma((BANDS,)),
-                dma((BANDS, 3)), dma((BANDS, 3)), dma((BANDS,)), dma((BANDS,)),
+                dma((14,)), dma((2,)), dma((3,)), dma((3,)), dma((BANDS,)), dma((BANDS,)),
+                dma((BANDS, 3)), dma((BANDS, 3)), dma((BANDS, 2)), dma((BANDS, 2)),
                 dma((BANDS, 3)), dma((BANDS, 3)),
             ],
             compiler_params=pltpu.CompilerParams(

time: 44.1 us -> 41.9 us (0.950)
  the two profiles are of different devices: /device:TPU:168 before, /device:TPU:224 now
where the time goes in v4:
time: 41.9 us; the launch traced here: 41.8 us
  Pallas kernels  39.5 us (94%)
  local copies, waits for them, and re-layouts  2.29 us (5%)
    pallas_call x1, Pallas kernels, step(): pl.pallas_call(functools.partial(kernel, tm_count), out_shape=jax.ShapeDt...  39.5 us
    unnamed x1, local copies, waits for them, and re-layouts  2.29 us

profile of v4, /device:TPU:224, one launch (start us, length us, event | category | flops | bytes accessed | tf_op | source)
XLA Modules:
  0.0 41.8 jit_solution(16069393282368067463)
XLA Ops:
  0.0 39.5 %encoder_block.1 = bf16[16,8,16,256]{3,2,1,0:T(8,128)(2,1)} custom-call(bf16[16,8,16,256]{3,2,1,0:T(8,128)(2,1)} %x_hbm.1, f32[1,256]{1,0:T(1,128)} %bitcast.2, bf16[3,3,256,256]{3,2,1,0:T(8,128)(2,1)} %cs_hbm.1, bf16[3,256,256]{2,1,0:T(8,128)(2,1)} %ct_hbm.1, f32[1,256]{1,0:T(1,128)} %bitcast.3, bf16[256,256]{1,0:T(8,128)(2,1)} %wq_hbm.1, ...), custom_call_target="tpu_custom_call" | custom-call | tf_op jit(solution)/shard_map/encoder_block/pallas_call | solution.py:379
  39.5 2.3 %copy.11 = bf16[16,8,16,256]{3,2,1,0:T(8,128)(2,1)} copy(bf16[16,8,16,256]{3,2,1,0:T(8,128)(2,1)} %encoder_block.1) | data formatting | bytes 2097152

commit v5 on v4

--- a/solution.py
+++ b/solution.py
@@ -9,6 +9,7 @@
 
 RING = 4
 BANDS = 4
+LAG = 2
 MESH = pl.DeviceIdType.MESH
 F32 = jnp.float32
 BF16 = jnp.bfloat16
@@ -20,6 +21,11 @@
 
 def iota(shape, dim):
     return lax.broadcasted_iota(jnp.int32, shape, dim)
+
+
+def swap():
+    r, s = iota((256, 256), 0), iota((256, 256), 1)
+    return (((r >> 4) == (s & 15)) & ((r & 15) == (s >> 4))).astype(F32).astype(BF16)
 
 
 def kernel(
@@ -28,7 +34,7 @@
     out_hbm,
     xs, cs, ct, wqkv, wo,
     perm, pick, place, bias, hmask,
-    ext, xp, sp, hsend, hrecv, hidden, abuf, xall, qb, kb, vb, mb, mback, res, ov,
+    ext, xp, sp, hsend, hrecv, hidden, abuf, xall, qb, kb, vb, mb, mback, res,
     load_sem, store_sem, rim_send, rim_recv, th_send, th_recv,
     a1_send, a1_recv, fw_send, fw_recv, a2_send, a2_recv,
 ):
@@ -79,8 +85,7 @@
             device_id=where, device_id_type=MESH,
         )
 
-    r, s = iota((256, 256), 0), iota((256, 256), 1)
-    perm[...] = (((r >> 4) == (s & 15)) & ((r & 15) == (s >> 4))).astype(F32).astype(BF16)
+    perm[...] = swap()
     r, s = iota((32, 256), 0), iota((32, 256), 1)
     pick[...] = (s == (r & 15) * 16 + 14 + (r >> 4)).astype(F32).astype(BF16)
     r, s = iota((512, 32), 0), iota((512, 32), 1)
@@ -133,16 +138,19 @@
             ext.at[rim_y, rim_x], ext.at[9 * row, 17 * col],
             rim_send.at[1], rim_recv.at[1], diag,
         ),
+    ] + [
         remote(
-            ext.at[pl.ds(1, 8), rim_x], ext.at[pl.ds(1, 8), 17 * col],
-            rim_send.at[2], rim_recv.at[2], side,
-        ),
+            ext.at[pl.ds(first, rows), rim_x], ext.at[pl.ds(first, rows), 17 * col],
+            rim_send.at[i], rim_recv.at[i], side,
+        )
+        for i, first, rows in ((2, 1 + 3 * row, 5), (3, 6 - 5 * row, 3))
     ]
     rims[0].start()
     rims[1].start()
 
     norm_rows(1)
     rims[2].start()
+    rims[3].start()
     loads[8].wait()
     loads[9].wait()
 
@@ -201,32 +209,38 @@
             a1_send.at[band, k - 1], a1_recv.at[band, k - 1], ring_at(k),
         )
 
-    @pl.loop(0, BANDS)
-    def _(band):
-        for step, rim in ((1, 0), (2, 2), (3, 1)):
-            pl.when(band == step)(lambda rim=rim: rims[rim].wait())
-
-        conv(band)
-        pl.when(has_next)(lambda: tm_copy(band).start())
-
     def forward(band, part):
         return remote(
             xall.at[band, 4 + part], xall.at[band, part],
             fw_send.at[band, part], fw_recv.at[band, part], group_next,
         )
 
-    @pl.loop(0, BANDS)
-    def _(band):
-        with jax.named_scope("tm_wait"):
-            pl.when(has_prev)(lambda: tm_copy(band).wait_recv())
-        temporal(band)
+    def send_out(band):
         for k in (1, 2, 3):
             a1_copy(band, k).start()
-        xall[band, 2 + ring] = abuf[band, ring]
-        for part in (0, 1):
-            pl.when(has_group_next & (ring == part + 2))(
-                lambda part=part: forward(band, part).start()
-            )
+
+    @pl.loop(0, BANDS + LAG)
+    def _(i):
+        @pl.when(i < BANDS)
+        def _():
+            for step, rim in ((1, 0), (2, 2), (3, 1), (3, 3)):
+                pl.when(i == step)(lambda rim=rim: rims[rim].wait())
+
+            conv(i)
+            pl.when(has_next)(lambda: tm_copy(i).start())
+
+        @pl.when(i >= LAG)
+        def _():
+            band = i - LAG
+            with jax.named_scope("tm_wait"):
+                pl.when(has_prev)(lambda: tm_copy(band).wait_recv())
+            temporal(band)
+            pl.when(band < 2)(lambda: send_out(band))
+            xall[band, 2 + ring] = abuf[band, ring]
+            for part in (0, 1):
+                pl.when(has_group_next & (ring == part + 2))(
+                    lambda part=part: forward(band, part).start()
+                )
 
     def a2_copy(band, k):
         to = lax.rem(ring + k, RING)
@@ -300,6 +314,7 @@
 
     arrive(0, 3)
     arrive(0, 2)
+    send_out(2)
 
     @pl.loop(0, BANDS + 1)
     def _(i):
@@ -311,13 +326,12 @@
                 tokens = xall[i, 2:6].reshape(512, 256)
                 qb[i] = dot(tokens, wqkv[0]).astype(BF16).reshape(4, 8, 16, 256)
             keys_values(i, 2, 4)
-            attend(i, 1)
-            send_back(i, 1)
 
         @pl.when(i < BANDS - 1)
         def _():
             arrive(i + 1, 3)
             arrive(i + 1, 2)
+            pl.when(i == 0)(lambda: send_out(3))
 
         @pl.when(i >= 1)
         def _():
@@ -328,6 +342,17 @@
             keys_values(band, 0, 2)
             attend(band, 0)
             send_back(band, 0)
+
+        @pl.when(i < BANDS)
+        def _():
+            attend(i, 1)
+            send_back(i, 1)
+
+    def store(band):
+        rows, columns = (pl.ds(start, size) for start, size in zip(corner(band), (4, 8)))
+        return pltpu.make_async_copy(
+            res.at[rows, columns], out_hbm.at[rows, columns], store_sem.at[band]
+        )
 
     @pl.loop(0, BANDS)
     def _(band):
@@ -341,18 +366,8 @@
             total = total.astype(BF16).reshape(RING, 4, 2, 16, 256)
             for q in range(RING):
                 res[pl.ds(y0, 4), pl.ds(c0 + 2 * q, 2)] = total[q]
-
-    stores = []
-    for half in range(2):
-        with jax.named_scope("unperm"):
-            for y in range(4 * half, 4 * half + 4):
-                o = dot(perm[...], res[y].reshape(256, 256)).astype(BF16)
-                ov[:, y] = o.reshape(16, 16, 256)
-        rows = pl.ds(4 * half, 4)
-        stores.append(
-            pltpu.make_async_copy(ov.at[:, rows], out_hbm.at[:, rows], store_sem.at[half])
-        )
-        stores[half].start()
+        store(band).start()
+
     @pl.loop(0, BANDS)
     def _(band):
         pl.when(has_next)(lambda: tm_copy(band).wait_send())
@@ -361,9 +376,30 @@
         for k in (1, 2, 3):
             a1_copy(band, k).wait_send()
 
-    with jax.named_scope("store"):
-        for store in stores:
-            store.wait()
+        store(band).wait()
+
+
+def reorder(y_hbm, out_hbm, perm, res, ov, load_sem, store_sem):
+    parts = [pl.ds(2 * i, 2) for i in range(4)]
+    loads = [
+        pltpu.make_async_copy(y_hbm.at[rows], res.at[rows], load_sem.at[i])
+        for i, rows in enumerate(parts)
+    ]
+    stores = [
+        pltpu.make_async_copy(ov.at[:, rows], out_hbm.at[:, rows], store_sem.at[i])
+        for i, rows in enumerate(parts)
+    ]
+    for load in loads:
+        load.start()
+    perm[...] = swap()
+    for i in range(4):
+        loads[i].wait()
+        for y in (2 * i, 2 * i + 1):
+            o = dot(perm[...], res[y].reshape(256, 256)).astype(BF16)
+            ov[:, y] = o.reshape(16, 16, 256)
+        stores[i].start()
+    for store in stores:
+        store.wait()
 
 
 def solution(mesh):
@@ -376,9 +412,9 @@
         dma = pltpu.SemaphoreType.DMA
         anywhere = pl.BlockSpec(memory_space=pltpu.HBM)
         here = pl.BlockSpec(memory_space=pltpu.VMEM)
-        return pl.pallas_call(
+        made = pl.pallas_call(
             functools.partial(kernel, tm_count),
-            out_shape=jax.ShapeDtypeStruct(x.shape, x.dtype),
+            out_shape=jax.ShapeDtypeStruct((8, 16, 16, 256), BF16),
             in_specs=[
                 anywhere, here, anywhere, anywhere, here,
                 anywhere, anywhere, anywhere, anywhere,
@@ -394,8 +430,8 @@
                 vmem(BANDS, 4, 128, 256), vmem(BANDS, 6, 128, 256),
                 vmem(BANDS, 4, 8, 16, 256), vmem(BANDS, 6, 8, 16, 256),
                 vmem(BANDS, 6, 8, 16, 256), vmem(BANDS, 4, 128, 256),
-                vmem(BANDS, 4, 128, 256), vmem(8, 16, 16, 256), vmem(16, 8, 16, 256),
-                dma((14,)), dma((2,)), dma((3,)), dma((3,)), dma((BANDS,)), dma((BANDS,)),
+                vmem(BANDS, 4, 128, 256), vmem(8, 16, 16, 256),
+                dma((14,)), dma((BANDS,)), dma((4,)), dma((4,)), dma((BANDS,)), dma((BANDS,)),
                 dma((BANDS, 3)), dma((BANDS, 3)), dma((BANDS, 2)), dma((BANDS, 2)),
                 dma((BANDS, 3)), dma((BANDS, 3)),
             ],
@@ -407,6 +443,17 @@
             x, norm_gain.reshape(1, -1), conv_space, conv_time, attn_gain.reshape(1, -1),
             wq, wk, wv, wo,
         )
+        return pl.pallas_call(
+            reorder,
+            out_shape=jax.ShapeDtypeStruct(x.shape, x.dtype),
+            in_specs=[anywhere],
+            out_specs=anywhere,
+            scratch_shapes=[
+                vmem(256, 256), vmem(8, 16, 16, 256), vmem(16, 8, 16, 256), dma((4,)), dma((4,)),
+            ],
+            compiler_params=pltpu.CompilerParams(vmem_limit_bytes=60 << 20),
+            name="reorder",
+        )(made)
 
     tile = P("tm", "row", "col", None)
     return jax.shard_map(

time: 41.9 us -> 40.6 us (0.969)
  the two profiles are of different devices: /device:TPU:224 before, /device:TPU:32 now
where the time goes in v5:
time: 40.6 us; the launch traced here: 39.9 us
  Pallas kernels  39.9 us (98%)
    pallas_call x1, Pallas kernels, step(): pl.pallas_call(functools.partial(kernel, tm_count), out_shape=jax.ShapeDt...  37.2 us
    pallas_call x1, Pallas kernels, step(): pl.pallas_call(reorder, out_shape=jax.ShapeDtypeStruct(x.shape, x.dtype),...  2.63 us

profile of v5, /device:TPU:32, one launch (start us, length us, event | category | flops | bytes accessed | tf_op | source)
XLA Modules:
  0.0 39.9 jit_solution(13240720605491964130)
XLA Ops:
  0.0 37.2 %encoder_block.1.y_hbm = bf16[8,16,16,256]{3,2,1,0:T(8,128)(2,1)} custom-call(bf16[16,8,16,256]{3,2,1,0:T(8,128)(2,1)} %x_hbm.1, f32[1,256]{1,0:T(1,128)} %bitcast.2, bf16[3,3,256,256]{3,2,1,0:T(8,128)(2,1)} %cs_hbm.1, bf16[3,256,256]{2,1,0:T(8,128)(2,1)} %ct_hbm.1, f32[1,256]{1,0:T(1,128)} %bitcast.3, bf16[256,256]{1,0:T(8,128)(2,1)} %wq_hbm.1, ...), custom_call_target="tpu_custom_call" | custom-call | tf_op jit(solution)/shard_map/encoder_block/pallas_call | solution.py:415
  37.2 2.6 %reorder.1 = bf16[16,8,16,256]{3,2,1,0:T(8,128)(2,1)} custom-call(bf16[8,16,16,256]{3,2,1,0:T(8,128)(2,1)} %encoder_block.1.y_hbm), custom_call_target="tpu_custom_call" | custom-call | tf_op jit(solution)/shard_map/reorder/pallas_call | solution.py:446

commit v6 on v5

--- a/solution.py
+++ b/solution.py
@@ -66,7 +66,7 @@
             ]
         )
     ]
-    for load in loads:
+    for load in loads[:8]:
         load.start()
 
     barrier = pltpu.get_barrier_semaphore()
@@ -124,6 +124,8 @@
         for band in range(BANDS):
             xall[band, 0:2] = jnp.zeros((2, 128, 256), BF16)
 
+    for load in loads[8:]:
+        load.start()
     norm_rows(0)
     with jax.named_scope("barrier"):
         later = has_next.astype(jnp.int32) + has_group_next.astype(jnp.int32)
@@ -216,7 +218,7 @@
         )
 
     def send_out(band):
-        for k in (1, 2, 3):
+        for k in (2, 1, 3):
             a1_copy(band, k).start()
 
     @pl.loop(0, BANDS + LAG)
@@ -389,7 +391,7 @@
         pltpu.make_async_copy(ov.at[:, rows], out_hbm.at[:, rows], store_sem.at[i])
         for i, rows in enumerate(parts)
     ]
-    for load in loads:
+    for load in loads[:8]:
         load.start()
     perm[...] = swap()
     for i in range(4):

time: 40.6 us -> 41.2 us (1.015)
  the two profiles are of different devices: /device:TPU:32 before, /device:TPU:170 now
where the time goes in v6:
time: 41.2 us; the launch traced here: 41.1 us
  Pallas kernels  41.1 us (100%)
    pallas_call x1, Pallas kernels, step(): pl.pallas_call(functools.partial(kernel, tm_count), out_shape=jax.ShapeDt...  38.4 us
    pallas_call x1, Pallas kernels, step(): pl.pallas_call(reorder, out_shape=jax.ShapeDtypeStruct(x.shape, x.dtype),...  2.64 us

profile of v6, /device:TPU:170, one launch (start us, length us, event | category | flops | bytes accessed | tf_op | source)
XLA Modules:
  0.0 41.1 jit_solution(732318337035061978)
XLA Ops:
  0.0 38.4 %encoder_block.1.y_hbm = bf16[8,16,16,256]{3,2,1,0:T(8,128)(2,1)} custom-call(bf16[16,8,16,256]{3,2,1,0:T(8,128)(2,1)} %x_hbm.1, f32[1,256]{1,0:T(1,128)} %bitcast.2, bf16[3,3,256,256]{3,2,1,0:T(8,128)(2,1)} %cs_hbm.1, bf16[3,256,256]{2,1,0:T(8,128)(2,1)} %ct_hbm.1, f32[1,256]{1,0:T(1,128)} %bitcast.3, bf16[256,256]{1,0:T(8,128)(2,1)} %wq_hbm.1, ...), custom_call_target="tpu_custom_call" | custom-call | tf_op jit(solution)/shard_map/encoder_block/pallas_call | solution.py:417
  38.4 2.6 %reorder.1 = bf16[16,8,16,256]{3,2,1,0:T(8,128)(2,1)} custom-call(bf16[8,16,16,256]{3,2,1,0:T(8,128)(2,1)} %encoder_block.1.y_hbm), custom_call_target="tpu_custom_call" | custom-call | tf_op jit(solution)/shard_map/reorder/pallas_call | solution.py:448

commit v7 on v5

--- a/solution.py
+++ b/solution.py
@@ -125,6 +125,7 @@
             xall[band, 0:2] = jnp.zeros((2, 128, 256), BF16)
 
     norm_rows(0)
+    norm_rows(1)
     with jax.named_scope("barrier"):
         later = has_next.astype(jnp.int32) + has_group_next.astype(jnp.int32)
         pl.semaphore_wait(barrier, len(partners) + later)
@@ -148,7 +149,6 @@
     rims[0].start()
     rims[1].start()
 
-    norm_rows(1)
     rims[2].start()
     rims[3].start()
     loads[8].wait()

time: 40.6 us -> 40.4 us (level)
  no operation moved by 1% of the time
where the time goes in v7:
time: 40.4 us; the launch traced here: 39.6 us
  Pallas kernels  39.6 us (98%)
    pallas_call x1, Pallas kernels, step(): pl.pallas_call(functools.partial(kernel, tm_count), out_shape=jax.ShapeDt...  37 us
    pallas_call x1, Pallas kernels, step(): pl.pallas_call(reorder, out_shape=jax.ShapeDtypeStruct(x.shape, x.dtype),...  2.63 us

profile of v7, /device:TPU:32, one launch (start us, length us, event | category | flops | bytes accessed | tf_op | source)
XLA Modules:
  0.0 39.6 jit_solution(7307546402538218559)
XLA Ops:
  0.0 37.0 %encoder_block.1.y_hbm = bf16[8,16,16,256]{3,2,1,0:T(8,128)(2,1)} custom-call(bf16[16,8,16,256]{3,2,1,0:T(8,128)(2,1)} %x_hbm.1, f32[1,256]{1,0:T(1,128)} %bitcast.2, bf16[3,3,256,256]{3,2,1,0:T(8,128)(2,1)} %cs_hbm.1, bf16[3,256,256]{2,1,0:T(8,128)(2,1)} %ct_hbm.1, f32[1,256]{1,0:T(1,128)} %bitcast.3, bf16[256,256]{1,0:T(8,128)(2,1)} %wq_hbm.1, ...), custom_call_target="tpu_custom_call" | custom-call | tf_op jit(solution)/shard_map/encoder_block/pallas_call | solution.py:415
  37.0 2.6 %reorder.1 = bf16[16,8,16,256]{3,2,1,0:T(8,128)(2,1)} custom-call(bf16[8,16,16,256]{3,2,1,0:T(8,128)(2,1)} %encoder_block.1.y_hbm), custom_call_target="tpu_custom_call" | custom-call | tf_op jit(solution)/shard_map/reorder/pallas_call | solution.py:446

commit v8 on v7

--- a/solution.py
+++ b/solution.py
@@ -216,7 +216,7 @@
         )
 
     def send_out(band):
-        for k in (1, 2, 3):
+        for k in (2, 1, 3):
             a1_copy(band, k).start()
 
     @pl.loop(0, BANDS + LAG)

time: 40.4 us -> 40.5 us (level)
  no operation moved by 1% of the time
where the time goes in v8:
time: 40.5 us; the launch traced here: 39.9 us
  Pallas kernels  39.9 us (99%)
    pallas_call x1, Pallas kernels, step(): pl.pallas_call(functools.partial(kernel, tm_count), out_shape=jax.ShapeDt...  37.3 us
    pallas_call x1, Pallas kernels, step(): pl.pallas_call(reorder, out_shape=jax.ShapeDtypeStruct(x.shape, x.dtype),...  2.65 us

profile of v8, /device:TPU:32, one launch (start us, length us, event | category | flops | bytes accessed | tf_op | source)
XLA Modules:
  0.0 39.9 jit_solution(10664380128258725800)
XLA Ops:
  0.0 37.3 %encoder_block.1.y_hbm = bf16[8,16,16,256]{3,2,1,0:T(8,128)(2,1)} custom-call(bf16[16,8,16,256]{3,2,1,0:T(8,128)(2,1)} %x_hbm.1, f32[1,256]{1,0:T(1,128)} %bitcast.2, bf16[3,3,256,256]{3,2,1,0:T(8,128)(2,1)} %cs_hbm.1, bf16[3,256,256]{2,1,0:T(8,128)(2,1)} %ct_hbm.1, f32[1,256]{1,0:T(1,128)} %bitcast.3, bf16[256,256]{1,0:T(8,128)(2,1)} %wq_hbm.1, ...), custom_call_target="tpu_custom_call" | custom-call | tf_op jit(solution)/shard_map/encoder_block/pallas_call | solution.py:415
  37.3 2.6 %reorder.1 = bf16[16,8,16,256]{3,2,1,0:T(8,128)(2,1)} custom-call(bf16[8,16,16,256]{3,2,1,0:T(8,128)(2,1)} %encoder_block.1.y_hbm), custom_call_target="tpu_custom_call" | custom-call | tf_op jit(solution)/shard_map/reorder/pallas_call | solution.py:446
